TPU v7x, 768 devices: a whole 4x8x12 slice. The times are simulated.
768 devices in a mesh: dp: 48 (over z, y_lo), mp: 16 (over y_hi, x, core).
Axes of the slice: x: 4, y: 8 (y_hi: 2, y_lo: 4; y = y_hi * 4 + y_lo), z: 12, core: 2. Of those that a mesh axis runs over, the one named last changes fastest.
Arguments:
- patches: bfloat16 [1152, 36864], P('mp', 'dp'), may hold values from -40 to 40
- counts: int32 [2304], replicated, may hold values from 4 to 16, as said below
- dest: int32 [2304], replicated, may hold values from 0 to 47, as said below
- w_qkv: bfloat16 [3, 1152, 1152], P(None, 'mp'), may hold values from -4 to 4
- w_out: bfloat16 [1152, 1152], P('mp'), may hold values from -0.1875 to 0.1875
- text: bfloat16 [2304, 1152], P(('dp', 'mp')), may hold values from -6 to 6
Outputs:
- grad_image: float32 [2304, 1152], P('dp', 'mp')
- grad_text: float32 [2304, 1152], P(('dp', 'mp'))
Inputs may be any that keep to these rules, and one draw needn't show every extreme that they name: `counts`: every dp index holds 48 images; on some dp index every image that is sent to it has 16 patches. `dest`: entries s * 48 to s * 48 + 47 are a permutation of 0 to 47: every dp index sends exactly one image to every dp index.
All inputs are finite; a program needn't handle non-finite values.
Results may differ from a plain program's by a relative error of at most 0.0046.
Values may be sent and summed in bfloat16 or wider, within the bound.
A program may use at most 64 MiB of HBM per device.

v0:
```python
import math

import jax
import jax.numpy as jnp
from jax import lax
from jax.sharding import PartitionSpec as P

D = 1152
HD = 72
MAXP = 16


def from_behind(shard, axis, by):
    peers = lax.axis_size(axis)
    return lax.ppermute(shard, axis, [(i, (i + by) % peers) for i in range(peers)])


def softmax_rounded(scores):
    row_max = jnp.max(scores, axis=-1, keepdims=True)
    raised = jnp.exp(scores - row_max)
    return (raised / jnp.sum(raised, axis=-1, keepdims=True)).astype(jnp.bfloat16)


def on_device(patches, counts, dest, w_qkv, w_out, text):
    devices = lax.axis_size("dp")
    lane_count = lax.axis_size("mp")
    dp_index = lax.axis_index("dp")
    mp_index = lax.axis_index("mp")
    width_local = patches.shape[0]
    heads_width = w_qkv.shape[1]
    heads_local = heads_width // HD
    count_table = counts.reshape(devices, devices)
    dest_table = dest.reshape(devices, devices)
    targets = jnp.arange(devices, dtype=jnp.int32)
    position = jnp.arange(MAXP, dtype=jnp.int32)
    own_counts = lax.dynamic_index_in_dim(count_table, dp_index, 0, keepdims=False)
    own_dest = lax.dynamic_index_in_dim(dest_table, dp_index, 0, keepdims=False)
    own_starts = jnp.cumsum(own_counts) - own_counts
    chosen = own_dest[None, :] == targets[:, None]
    send_count = jnp.sum(jnp.where(chosen, own_counts[None, :], 0), axis=1)
    send_start = jnp.sum(jnp.where(chosen, own_starts[None, :], 0), axis=1)
    send_valid = position[None, :] < send_count[:, None]
    send_rows = jnp.where(send_valid, send_start[:, None] + position[None, :], 0)
    picked = jnp.take(patches, send_rows.reshape(-1), axis=1).reshape(width_local, devices, MAXP)
    picked = jnp.where(send_valid[None, :, :], picked, jnp.zeros((), jnp.bfloat16))
    outgoing = jnp.transpose(picked, (1, 0, 2)).reshape(devices, width_local * MAXP)
    received = lax.all_to_all(outgoing, "dp", split_axis=0, concat_axis=0, tiled=True)
    arrived = dest_table == dp_index
    got_count = jnp.sum(jnp.where(arrived, count_table, 0), axis=1)
    got_index = jnp.sum(jnp.where(arrived, targets[None, :], 0), axis=1)
    image_ids = targets * devices + got_index
    counts_float = got_count.astype(jnp.float32)[:, None]
    rows_float = received.reshape(devices, width_local, MAXP).astype(jnp.float32)
    slice_mean = jnp.sum(rows_float, axis=2) / counts_float
    gathered = lax.all_gather(received, "mp", axis=1, tiled=True)
    full_float = gathered.reshape(devices, D, MAXP).astype(jnp.float32)
    row_mean = jnp.mean(full_float, axis=1, keepdims=True)
    centred = full_float - row_mean
    row_var = jnp.mean(centred * centred, axis=1, keepdims=True)
    normed = (centred * lax.rsqrt(row_var + 1e-06)).astype(jnp.bfloat16)
    projected = jnp.einsum("sdp,chd->csph", normed, w_qkv, preferred_element_type=jnp.float32)
    projected = projected.astype(jnp.bfloat16).reshape(3, devices, MAXP, heads_local, HD)
    query, key_rows, value = (projected[0], projected[1], projected[2])
    total_rows = devices * MAXP
    slot_ends = jnp.cumsum(got_count)
    slot_starts = slot_ends - got_count
    packed_row = jnp.arange(total_rows, dtype=jnp.int32)
    segment_of = jnp.sum((packed_row[:, None] >= slot_ends[None, :]).astype(jnp.int32), axis=1)
    live_row = packed_row < slot_ends[devices - 1]
    member = (segment_of[:, None] == targets[None, :]) & live_row[:, None]
    row_start = jnp.sum(jnp.where(member, slot_starts[None, :], 0), axis=1)
    source_row = jnp.where(live_row, segment_of * MAXP + packed_row - row_start, 0)
    segment_id = jnp.where(live_row, segment_of, -1)
    query_rows = query.reshape(total_rows, heads_local, HD)[source_row]
    key_packed = key_rows.reshape(total_rows, heads_local, HD)[source_row]
    value_packed = value.reshape(total_rows, heads_local, HD)[source_row]
    tile_rows = math.gcd(total_rows, 512)
    tile_count = total_rows // tile_rows
    window = min(tile_rows + 2 * MAXP, total_rows)

    def attend_tile(item):
        tile_index, query_tile, segment_tile = item
        window_start = jnp.clip(tile_index * tile_rows - MAXP, 0, total_rows - window)
        key_window = lax.dynamic_slice_in_dim(key_packed, window_start, window, 0)
        value_window = lax.dynamic_slice_in_dim(value_packed, window_start, window, 0)
        segment_window = lax.dynamic_slice_in_dim(segment_id, window_start, window, 0)
        scores = jnp.einsum(
            "phd,qhd->hpq", query_tile, key_window, preferred_element_type=jnp.float32
        ) / math.sqrt(HD)
        same_image = segment_tile[:, None] == segment_window[None, :]
        scores = jnp.where(same_image[None, :, :], scores, -1e30)
        weights = softmax_rounded(scores)
        return jnp.einsum(
            "hpq,qhd->phd", weights, value_window, preferred_element_type=jnp.float32
        ).astype(jnp.bfloat16)

    tile_numbers = jnp.arange(tile_count, dtype=jnp.int32)
    mixed = lax.map(
        attend_tile,
        (
            tile_numbers,
            query_rows.reshape(tile_count, tile_rows, heads_local, HD),
            segment_id.reshape(tile_count, tile_rows),
        ),
    )
    mixed = mixed.reshape(total_rows, heads_width)
    summed = jnp.einsum(
        "rs,rh->sh", member.astype(jnp.bfloat16), mixed, preferred_element_type=jnp.float32
    )
    pooled_heads = (summed / counts_float).astype(jnp.bfloat16)
    pool_term = jnp.dot(pooled_heads, w_out, preferred_element_type=jnp.float32)
    start_column = mp_index * width_local
    own_columns = lax.dynamic_slice_in_dim(pool_term, start_column, width_local, 1) + slice_mean
    pool_term = lax.dynamic_update_slice(
        pool_term, own_columns, (jnp.zeros((), jnp.int32), start_column)
    )
    pooled = lax.psum(pool_term, "mp")
    image_unit = (
        pooled * lax.rsqrt(jnp.sum(pooled * pooled, axis=-1, keepdims=True) + 1e-06)
    ).astype(jnp.bfloat16)
    text_float = text.astype(jnp.float32)
    text_unit = (
        text_float * lax.rsqrt(jnp.sum(text_float * text_float, axis=-1, keepdims=True) + 1e-06)
    ).astype(jnp.bfloat16)
    texts_here = text.shape[0]
    text_offsets = jnp.arange(texts_here, dtype=jnp.int32)

    def pair_turn(step_index, carried):
        travelling, text_grads, image_partial = carried
        anchor = (dp_index - step_index) % devices
        text_ids = (anchor * lane_count + mp_index) * texts_here + text_offsets
        travelling_bf = travelling.astype(jnp.bfloat16)
        logits = (
            4.0
            * jnp.einsum("ad,jd->aj", image_unit, travelling_bf, preferred_element_type=jnp.float32)
            - 2.0
        )
        labels = jnp.where(image_ids[:, None] == text_ids[None, :], 1.0, -1.0)
        dscaled = (-4.0 * labels * jax.nn.sigmoid(-labels * logits)).astype(jnp.bfloat16)
        image_partial = image_partial + jnp.einsum(
            "aj,jd->ad", dscaled, travelling_bf, preferred_element_type=jnp.float32
        )
        text_grads = text_grads + jnp.einsum(
            "aj,ad->jd", dscaled, image_unit, preferred_element_type=jnp.float32
        )
        travelling, text_grads = from_behind((travelling, text_grads), "dp", 1)
        return (travelling, text_grads, image_partial)

    initial = (
        text_unit.astype(jnp.float32),
        jnp.zeros((texts_here, D), jnp.float32),
        jnp.zeros((devices, D), jnp.float32),
    )
    travelling, text_grads, image_partial = lax.fori_loop(0, devices, pair_turn, initial)
    grad_image = lax.psum_scatter(image_partial, "mp", scatter_dimension=1, tiled=True)
    return (grad_image, text_grads)


def solution(mesh):
    placed = (P("mp", "dp"), P(), P(), P(None, "mp", None), P("mp", None), P(("dp", "mp"), None))
    return jax.shard_map(
        on_device,
        mesh=mesh,
        in_specs=placed,
        out_specs=(P("dp", "mp"), P(("dp", "mp"), None)),
        check_vma=False,
    )
```

profile of v0, /device:TPU:1, one launch (start us, length us, event | category | flops | bytes accessed | tf_op | source)
XLA Modules:
  0.0 1097.1 jit_solution(14897352824500013816)
XLA Ops:
  14.8 31.3 %all_to_all.12 = bf16[48,2,576]{2,1,0:T(2,128)(2,1)S(1)} all-to-all(bf16[48,2,576]{2,1,0:T(2,128)(2,1)S(1)} %reshape.342), channel_id=1, replica_groups=mesh['dp'=48,'mp'=16] {'dp'}, dimensions={0} | all-to-all | bytes 221184 | tf_op jit(solution)/shard_map/all_to_all | solution.py:47
  53.3 58.1 %all-gather.3.cloned.1.call-done = bf16[48,1,18432]{2,0,1:T(8,128)(2,1)} async-done(((bf16[48,1,1152]{2,0,1:T(8,128)(2,1)}), bf16[48,1,18432]{2,0,1:T(8,128)(2,1)}) %all-gather.3.cloned.1.call-update) | async-done | bytes 1769488 | tf_op jit(solution)/shard_map/all_gather | solution.py:55
  111.4 6.1 copy.58
  117.4 4.4 reduce_sum.118
  121.8 4.4 multiply_reduce_fusion
  126.3 5.8 fusion.24
  132.1 8.1 copy.67
  147.5 6.4 while.32
  155.8 180.5 %all-reduce.4.cloned.1.call-done = f32[48,1152]{1,0:T(8,128)} async-done(((f32[48,1152]{1,0:T(8,128)}), f32[48,1152]{1,0:T(8,128)}) %all-reduce.4.cloned.1.call-update) | async-done | bytes 221200 | tf_op jit(solution)/shard_map/psum | solution.py:117
  338.4 513.5 %while.33 = (s32[]{:T(128)}, bf16[3,1152]{1,0:T(4,128)(2,1)S(1)}, f32[3,1152]{1,0:T(4,128)S(1)}, f32[48,1152]{1,0:T(8,128)S(1)}, s32[48]{0:T(128)S(1)}, /*index=...) while((s32[]{:T(128)}, bf16[3,1152]{1,0:T(4,128)(2,1)S(1)}, ...), condition=%wide.region_19.20_spmd.clone, body=%wide.region_18.19_spmd.clone.sunk | while | flops 1111120 | bytes 803197 | solution.py:154
  375.2 3.9 collective-permute-done
  407.3 4.2 collective-permute-done
  428.6 4.2 collective-permute-done
  439.7 3.9 collective-permute-done
  461.1 3.9 collective-permute-done
  493.1 3.9 collective-permute-done
  525.1 3.9 collective-permute-done
  578.5 3.9 collective-permute-done
  610.5 3.9 collective-permute-done
  663.9 3.9 collective-permute-done
  695.9 3.9 collective-permute-done
  738.6 4.2 collective-permute-done
  759.9 4.2 collective-permute-done
  854.6 233.8 %all-reduce.6.cloned.1.call-done = f32[48,1152]{1,0:T(8,128)} async-done(((f32[48,1152]{1,0:T(8,128)}), f32[48,1152]{1,0:T(8,128)}) %all-reduce.6.cloned.1.call-update) | async-done | bytes 221200
  (521 shorter events, 492.9 us)
Async XLA Ops:
  7.2 104.2 %all-gather.3.cloned.1.call-start = ((), (), s32[]{:S(2)}) async-start(), calls=%async_computation.2 | async-start | bytes 1880064 | tf_op jit(solution)/shard_map/all_gather | solution.py:55
  46.9 289.4 %all-reduce.4.cloned.1.call-start = ((), (), s32[]{:S(2)}) async-start(), calls=%async_computation.1 | async-start | bytes 442368 | tf_op jit(solution)/shard_map/psum | solution.py:117
  155.7 932.7 %all-reduce.6.cloned.1.call-start = ((), (), s32[]{:S(2)}) async-start(), calls=%async_computation.3 | async-start | bytes 442368
  341.0 8.4 collective-permute-start.1
  351.7 8.4 collective-permute-start.1
  362.4 8.4 collective-permute-start.1
  373.1 8.4 collective-permute-start.1
  383.7 8.4 collective-permute-start.1
  394.4 8.4 collective-permute-start.1
  402.8 8.7 collective-permute-start
  405.1 8.4 collective-permute-start.1
  415.7 8.4 collective-permute-start.1
  424.2 8.6 collective-permute-start
  426.4 8.8 collective-permute-start.1
  437.5 8.4 collective-permute-start.1
  448.2 8.4 collective-permute-start.1
  458.9 8.4 collective-permute-start.1
  469.5 8.4 collective-permute-start.1
  480.2 8.4 collective-permute-start.1
  522.9 8.4 collective-permute-start.1
  683.0 8.4 collective-permute-start.1
  734.1 8.7 collective-permute-start
  755.5 8.6 collective-permute-start
  757.7 8.8 collective-permute-start.1
  (79 other events, 773.0 us)
Sparse Core Ops, SparseCore 0:
  47.0 64.2 all-gather.2
  155.9 180.4 all-reduce.3
  852.8 235.6 all-reduce.5
where the time goes:
time: 1100 us
  waiting for transfers between devices  772 us (70%)
  starting transfers between devices  184 us (17%)
  local copies, waits for them, and re-layouts  36.8 us (3%)
  blocking collectives  31.3 us (3%)
  matrix products  29.7 us (3%)
  other arithmetic  23.2 us (2%)
  between operations  14.8 us (1%)
    ppermute x96, waiting for transfers between devices, from_behind(): lax.ppermute(shard, axis, [(i, (i + by) % peers) for i in range(peers)])  299 us
    unnamed x4, waiting for transfers between devices  234 us
    ppermute x96, starting transfers between devices, from_behind(): lax.ppermute(shard, axis, [(i, (i + by) % peers) for i in range(peers)])  184 us
    psum x1, waiting for transfers between devices, on_device(): pooled = lax.psum(pool_term, 'mp')  181 us
    all_gather x1, waiting for transfers between devices, on_device(): gathered = lax.all_gather(received, 'mp', axis=1, tiled=True)  58.1 us
    all_to_all x1, blocking collectives, on_device(): lax.all_to_all(outgoing, 'dp', split_axis=0, concat_axis=0, tiled=True)  31.3 us
  transfers between devices with their start and end apart: 99, of which 99 were waited for; matrix products, arithmetic and copies ran while one was open for 3% of the time, Pallas kernels for 0%

commit v1 on v0

v1 whole, which is shorter than its diff:
```python
import math

import jax
import jax.numpy as jnp
from jax import lax
from jax.experimental import pallas as pl
from jax.experimental.pallas import tpu as pltpu
from jax.sharding import PartitionSpec as P

HD = 72
MAXP = 16
NYL = 4
NYH = 2
NX = 4
NG = NYH * NX
LANES = 128
F32 = jnp.float32
BF16 = jnp.bfloat16
MESH = pl.DeviceIdType.MESH


def iota(shape, dim):
    return lax.broadcasted_iota(jnp.int32, shape, dim)


def dot_nn(a, b):
    return lax.dot_general(a, b, (((1,), (0,)), ((), ())), preferred_element_type=F32)


def dot_nt(a, b):
    return lax.dot_general(a, b, (((1,), (1,)), ((), ())), preferred_element_type=F32)


def make_kernel(dp_size, width, texts_here):
    nz = dp_size // NYL
    half = dp_size // 2
    images_here = half // NG
    pieces = width // LANES
    used = images_here * pieces
    packed = -(-used // 16) * 16
    slots = dp_size * MAXP
    half_slots = half * MAXP
    plane = NYL * NG
    rows = NYL * half
    text_rows = texts_here * 2 * nz
    wide = -(-(4 * HD) // LANES) * LANES

    def kernel(
        counts,
        dest,
        patches,
        w_qkv,
        w_out,
        text,
        grad_image,
        grad_text,
        outbox,
        inbox,
        w_qkv_peer,
        w_out_peer,
        feats,
        text_f,
        text_box,
        text_in,
        text_wide,
        text_full,
        text_pad,
        part_f,
        part_b,
        part_in,
        mean_f,
        unit_box,
        unit_in,
        unit_wide,
        unit_full,
        gi_box,
        gi_in,
        gi_sum,
        gy_box,
        gy_in,
        gt_f,
        gt_in,
        gt_box,
        gtz_in,
        local_sem,
        a2a_send,
        a2a_recv,
        w_send,
        w_recv,
        g_send,
        g_recv,
        text_send,
        text_recv,
        part_send,
        part_recv,
        unit_send,
        unit_recv,
        gi_send,
        gi_recv,
        gy_send,
        gy_recv,
        gt_send,
        gt_recv,
        gtz_send,
        gtz_recv,
    ):
        me = lax.axis_index("dp")
        mp = lax.axis_index("mp")
        g, c = mp // 2, mp % 2
        z, ylo = me // NYL, me % NYL
        yhi, x = g // NX, g % NX
        y = yhi * NYL + ylo
        other = 1 - c
        partner = (me, g * 2 + other)
        my_half = me // half
        my_slot = me % half
        extra = jnp.where(my_half == c, 0, 1)

        barrier = pltpu.get_barrier_semaphore()

        def greet(device):
            pl.semaphore_signal(barrier, inc=1, device_id=device, device_id_type=MESH)

        @pl.loop(0, half)
        def _(i):
            src = half * c + i
            greet((src, g * 2 + other))

            @pl.when(src != me)
            def _():
                greet((src, mp))

        greet(partner)

        @pl.loop(1, nz)
        def _(i):
            zz = lax.rem(z + i, nz)
            greet((zz * NYL + ylo, g * 2))
            greet((zz * NYL + ylo, g * 2 + 1))

        place = ylo * NG + g

        @pl.loop(1, plane)
        def _(i):
            q = lax.rem(place + i, plane)
            greet((z * NYL + q // NG, (q % NG) * 2 + c))

        @pl.loop(1, 2 * NYL)
        def _(i):
            q = lax.rem(y + i, 2 * NYL)
            greet((z * NYL + q % NYL, ((q // NYL) * NX + x) * 2 + other))

        own_counts = counts[pl.ds(me, 1), :]
        own_dest = dest[pl.ds(me, 1), :]
        lane = iota((slots, dp_size), 1)
        target = iota((slots, dp_size), 0) // MAXP
        index = jnp.sum(jnp.where(own_dest == target, lane, 0), axis=1, keepdims=True)
        start = jnp.sum(jnp.where(lane < index, own_counts, 0), axis=1, keepdims=True)
        count = jnp.sum(jnp.where(lane == index, own_counts, 0), axis=1, keepdims=True)
        position = iota((slots, 1), 0) % MAXP
        column = jnp.where(position < count, start + position, -1)
        chosen = (iota((slots, patches.shape[1]), 1) == column).astype(F32).astype(BF16)
        picked = dot_nt(chosen, patches[...]).astype(BF16)
        outbox[...] = picked.reshape(dp_size, MAXP, HD)

        total = (2 * half - 1 + extra) + 1 + 2 * (nz - 1) + (plane - 1) + (2 * NYL - 1)
        pl.semaphore_wait(barrier, total)

        def image_copy(d):
            return pltpu.make_async_remote_copy(
                src_ref=outbox.at[d],
                dst_ref=inbox.at[c * half + my_slot],
                send_sem=a2a_send,
                recv_sem=a2a_recv,
                device_id=(d, g * 2 + my_half),
                device_id_type=MESH,
            )

        @pl.loop(1, dp_size)
        def _(i):
            image_copy(lax.rem(me + i, dp_size)).start()

        own_copy = pltpu.make_async_copy(
            outbox.at[me], inbox.at[c * half + my_slot], local_sem
        )

        @pl.when(my_half == c)
        def _():
            own_copy.start()

        @pl.when(my_half != c)
        def _():
            image_copy(me).start()

        def swap(src, dst, i):
            return pltpu.make_async_remote_copy(
                src_ref=src,
                dst_ref=dst,
                send_sem=w_send.at[i],
                recv_sem=w_recv.at[i],
                device_id=partner,
                device_id_type=MESH,
            )

        swap_qkv = swap(w_qkv, w_qkv_peer, 0)
        swap_out = swap(w_out, w_out_peer, 1)
        swap_qkv.start()
        swap_out.start()

        text_float = text[...].astype(F32)
        text_unit = text_float * lax.rsqrt(
            jnp.sum(text_float * text_float, axis=1, keepdims=True) + 1e-6
        )
        text_f[...] = jnp.zeros_like(text_f)
        for t in range(texts_here):
            for k in range(pieces):
                text_f[t * pieces + k : t * pieces + k + 1, :] = text_unit[
                    t : t + 1, k * LANES : (k + 1) * LANES
                ]
        own_text = text_f[...].astype(BF16)
        text_box[...] = own_text
        text_in[c * nz + z] = own_text

        def text_copy(zz, core):
            return pltpu.make_async_remote_copy(
                src_ref=text_box,
                dst_ref=text_in.at[c * nz + z],
                send_sem=text_send,
                recv_sem=text_recv,
                device_id=(zz * NYL + ylo, g * 2 + core),
                device_id_type=MESH,
            )

        text_copy(z, other).start()

        @pl.loop(1, nz)
        def _(i):
            zz = lax.rem(z + i, nz)
            text_copy(zz, 0).start()
            text_copy(zz, 1).start()

        mine = pl.ds(pl.multiple_of(half * c, 8), half)
        got = jnp.sum(
            jnp.where(dest[mine, :] == me, counts[mine, :], 0), axis=1, keepdims=True
        )

        @pl.when(my_half == c)
        def _():
            own_copy.wait()
            pltpu.make_async_remote_copy(
                src_ref=inbox.at[pl.ds(0, 2 * half - 1)],
                dst_ref=inbox.at[pl.ds(0, 2 * half - 1)],
                send_sem=a2a_send,
                recv_sem=a2a_recv,
                device_id=partner,
                device_id_type=MESH,
            ).wait_recv()

        @pl.when(my_half != c)
        def _():
            pltpu.make_async_remote_copy(
                src_ref=inbox,
                dst_ref=inbox,
                send_sem=a2a_send,
                recv_sem=a2a_recv,
                device_id=partner,
                device_id_type=MESH,
            ).wait_recv()

        eye = (iota((HD, HD), 0) == iota((HD, HD), 1)).astype(F32).astype(BF16)
        low = dot_nt(eye, inbox[0:half].reshape(half_slots, HD))
        high = dot_nt(eye, inbox[half : 2 * half].reshape(half_slots, HD))
        block = jnp.concatenate([low, high], axis=0).astype(BF16)
        for k in range(images_here):
            feats[k, g] = block[:, k * LANES : (k + 1) * LANES]

        across = (1 - yhi) * NX + x
        left_x, right_x = lax.rem(x + NX - 1, NX), lax.rem(x + 1, NX)
        far_x = lax.rem(x + 2, NX)

        def feat_copy(k, owner, to):
            return pltpu.make_async_remote_copy(
                src_ref=feats.at[k, owner],
                dst_ref=feats.at[k, owner],
                send_sem=g_send.at[k],
                recv_sem=g_recv.at[k, owner],
                device_id=(me, to * 2 + c),
                device_id_type=MESH,
            )

        own_row, far_row = yhi * NX, (1 - yhi) * NX
        left, right = own_row + left_x, own_row + right_x
        for k in range(images_here):
            feat_copy(k, g, across).start()
            feat_copy(k, g, left).start()
            feat_copy(k, g, right).start()

        def relay(k, row, flip):
            feat_copy(k, row + left_x, left).wait_recv()
            if not flip:
                feat_copy(k, row + left_x, right).start()
            feat_copy(k, row + right_x, left).wait_recv()
            if flip:
                feat_copy(k, row + right_x, left).start()

        for k in range(images_here):
            relay(k, own_row, k % 2 == 1)
            feat_copy(k, across, across).wait_recv()
            feat_copy(k, across, left).start()
            feat_copy(k, across, right).start()

        swap_qkv.wait()
        swap_out.wait()

        part_f[...] = jnp.zeros_like(part_f)
        mean_f[...] = jnp.zeros_like(mean_f)
        row8, lane8 = iota((NG, LANES), 0), iota((NG, LANES), 1)
        same = iota((LANES, LANES), 0) // MAXP == iota((LANES, LANES), 1) // MAXP
        for k in range(images_here):
            relay(k, far_row, k % 2 == 0)
            feat_copy(k, own_row + far_x, left).wait_recv()
            feat_copy(k, far_row + far_x, left).wait_recv()
            raw = feats[k].reshape(width, LANES)
            full = raw.astype(F32)
            centred = full - jnp.sum(full, axis=0, keepdims=True) / width
            variance = jnp.sum(centred * centred, axis=0, keepdims=True) / width
            normed = (centred * lax.rsqrt(variance + 1e-6)).astype(BF16)
            got_k = got[k * NG : (k + 1) * NG]
            got_float = got_k.astype(F32)
            real = (lane8 // MAXP == row8) & (lane8 % MAXP < got_k)
            real_float = real.astype(F32)
            key_real = jnp.max(real_float, axis=0, keepdims=True) > 0.5
            member = real_float.astype(BF16)
            keep = same & key_real
            term = jnp.zeros((NG, width), F32)
            for wq, wo in ((w_qkv, w_out), (w_qkv_peer, w_out_peer)):
                projected = dot_nn(wq[...], normed)
                query = jnp.transpose(projected[0:HD]).astype(BF16)
                key = projected[HD : 2 * HD].astype(BF16)
                value = projected[2 * HD : 3 * HD].astype(BF16)
                scores = dot_nn(query, key) / math.sqrt(HD)
                scores = jnp.where(keep, scores, -1e30)
                raised = jnp.exp(scores - jnp.max(scores, axis=1, keepdims=True))
                weights = (raised / jnp.sum(raised, axis=1, keepdims=True)).astype(BF16)
                mixed = dot_nt(value, weights).astype(BF16)
                pooled = (dot_nt(member, mixed) / got_float).astype(BF16)
                term = term + dot_nn(pooled, wo[...])
            for p in range(pieces):
                part_f[pl.ds(k * pieces + p, NG, stride=packed), :] = term[
                    :, p * LANES : (p + 1) * LANES
                ]
            here = (lane8 // MAXP == g).astype(F32).astype(BF16)
            own_got = jnp.sum(
                jnp.where(iota((NG, 1), 0) == g, got_float, 0.0), axis=0, keepdims=True
            )
            mean = dot_nt(here, raw) / own_got
            for p in range(pieces):
                r = k * pieces + p
                mean_f[r : r + 1, :] = mean[0:1, p * LANES : (p + 1) * LANES]

        part_b[...] = part_f[...].astype(BF16).reshape(NG, packed, LANES)

        def part_copy(gg):
            return pltpu.make_async_remote_copy(
                src_ref=part_b.at[gg],
                dst_ref=part_in.at[g],
                send_sem=part_send,
                recv_sem=part_recv,
                device_id=(me, gg * 2 + c),
                device_id_type=MESH,
            )

        @pl.loop(1, NG)
        def _(i):
            part_copy(lax.rem(g + i, NG)).start()

        part_in[g] = part_b[g]

        pltpu.make_async_remote_copy(
            src_ref=text_in.at[pl.ds(0, 2 * nz - 1)],
            dst_ref=text_in.at[pl.ds(0, 2 * nz - 1)],
            send_sem=text_send,
            recv_sem=text_recv,
            device_id=partner,
            device_id_type=MESH,
        ).wait()
        text_wide[...] = text_in[...].astype(F32).reshape(2 * nz * packed, LANES)
        for t in range(texts_here):
            for p in range(pieces):
                text_full[t * 2 * nz : (t + 1) * 2 * nz, p * LANES : (p + 1) * LANES] = (
                    text_wide[pl.ds(t * pieces + p, 2 * nz, stride=packed), :]
                )
        text_pad[...] = jnp.zeros_like(text_pad)
        for xx in range(NX):
            for q in range(4):
                m = ((q // 2) * NX + xx) * 2 + q % 2
                text_pad[:, xx * wide + q * HD : xx * wide + (q + 1) * HD] = text_full[
                    :, m * HD : (m + 1) * HD
                ]
        text_rows_b = text_full[...].astype(BF16)
        text_cols_b = text_pad[...].astype(BF16)

        part_seven = pltpu.make_async_remote_copy(
            src_ref=part_in.at[pl.ds(0, NG - 1)],
            dst_ref=part_in.at[pl.ds(0, NG - 1)],
            send_sem=part_send,
            recv_sem=part_recv,
            device_id=partner,
            device_id_type=MESH,
        )
        part_seven.wait()
        pooled = jnp.sum(part_in[...].astype(F32), axis=0) + mean_f[...]
        squares = jnp.sum(pooled * pooled, axis=1, keepdims=True)
        row_id = iota((packed, 1), 0)
        scale = jnp.zeros((packed, 1), F32)
        for k in range(images_here):
            inside = (row_id >= k * pieces) & (row_id < (k + 1) * pieces)
            norm = jnp.sum(jnp.where(inside, squares, 0.0), axis=0, keepdims=True)
            scale = jnp.where(inside, lax.rsqrt(norm + 1e-6), scale)
        own_unit = (pooled * scale).astype(BF16)
        unit_box[...] = own_unit
        unit_in[place] = own_unit

        def unit_copy(q):
            return pltpu.make_async_remote_copy(
                src_ref=unit_box,
                dst_ref=unit_in.at[place],
                send_sem=unit_send,
                recv_sem=unit_recv,
                device_id=(z * NYL + q // NG, (q % NG) * 2 + c),
                device_id_type=MESH,
            )

        @pl.loop(1, plane)
        def _(i):
            unit_copy(lax.rem(place + i, plane)).start()

        pltpu.make_async_remote_copy(
            src_ref=unit_in.at[pl.ds(0, plane - 1)],
            dst_ref=unit_in.at[pl.ds(0, plane - 1)],
            send_sem=unit_send,
            recv_sem=unit_recv,
            device_id=partner,
            device_id_type=MESH,
        ).wait()
        unit_wide[...] = unit_in[...].astype(F32).reshape(plane * packed, LANES)
        for yy in range(NYL):
            for k in range(images_here):
                for p in range(pieces):
                    unit_full[
                        yy * half + k * NG : yy * half + (k + 1) * NG,
                        p * LANES : (p + 1) * LANES,
                    ] = unit_wide[
                        pl.ds(yy * NG * packed + k * pieces + p, NG, stride=packed), :
                    ]
        units = unit_full[...].astype(BF16)

        text_id = iota((text_rows, dp_size), 0)
        text_z = text_id % nz
        text_core = (text_id % (2 * nz)) // nz
        text_t = text_id // (2 * nz)
        col = iota((text_rows, dp_size), 1)
        source = (col == text_z * NYL + ylo).astype(F32).astype(BF16)
        dest_rows = dot_nn(source, dest[...].astype(F32).astype(BF16))
        pair_col = (g * 2 + text_core) * texts_here + text_t
        pair_dest = jnp.sum(
            jnp.where(col == pair_col, dest_rows, 0.0), axis=1, keepdims=True
        ).astype(jnp.int32)
        image_lane = iota((text_rows, rows), 1)
        image_source = c * half + image_lane % half
        image_dest = z * NYL + image_lane // half
        text_source = (iota((text_rows, 1), 0) % nz) * NYL + ylo
        paired = (image_source == text_source) & (image_dest == pair_dest)
        labels = jnp.where(paired, 1.0, -1.0)
        logits = 4.0 * dot_nt(text_rows_b, units) - 2.0
        dscaled = -4.0 * labels / (1.0 + jnp.exp(labels * logits))
        turned = jnp.transpose(dscaled).astype(BF16)
        dscaled = dscaled.astype(BF16)

        text_grad = dot_nn(dscaled, units)
        gt_f[...] = jnp.zeros_like(gt_f)
        for t in range(texts_here):
            for p in range(pieces):
                gt_f[pl.ds(t * pieces + p, 2 * nz, stride=packed), :] = text_grad[
                    t * 2 * nz : (t + 1) * 2 * nz, p * LANES : (p + 1) * LANES
                ]
        core_rows = nz * packed
        gt_copy = pltpu.make_async_remote_copy(
            src_ref=gt_f.at[pl.ds(pl.multiple_of(other * core_rows, 8), core_rows)],
            dst_ref=gt_in,
            send_sem=gt_send,
            recv_sem=gt_recv,
            device_id=partner,
            device_id_type=MESH,
        )
        gt_copy.start()

        for xx in range(NX):
            gi_box[xx] = dot_nn(turned, text_cols_b[:, xx * wide : (xx + 1) * wide]).astype(BF16)

        def gi_copy(xx):
            return pltpu.make_async_remote_copy(
                src_ref=gi_box.at[xx],
                dst_ref=gi_in.at[x],
                send_sem=gi_send,
                recv_sem=gi_recv,
                device_id=(me, (yhi * NX + xx) * 2 + c),
                device_id_type=MESH,
            )

        for i in range(1, NX):
            gi_copy(lax.rem(x + i, NX)).start()
        gi_in[x] = gi_box[x]

        gt_copy.wait()
        own_rows = gt_f[pl.ds(pl.multiple_of(c * core_rows, 8), core_rows), :]
        gt_box[...] = (own_rows + gt_in[...]).astype(BF16).reshape(nz, packed, LANES)

        def gtz_copy(zz):
            return pltpu.make_async_remote_copy(
                src_ref=gt_box.at[zz],
                dst_ref=gtz_in.at[z],
                send_sem=gtz_send,
                recv_sem=gtz_recv,
                device_id=(zz * NYL + ylo, mp),
                device_id_type=MESH,
            )

        @pl.loop(1, nz)
        def _(i):
            gtz_copy(lax.rem(z + i, nz)).start()

        gtz_in[z] = gt_box[z]

        pltpu.make_async_remote_copy(
            src_ref=gi_in.at[pl.ds(0, NX - 1)],
            dst_ref=gi_in.at[pl.ds(0, NX - 1)],
            send_sem=gi_send,
            recv_sem=gi_recv,
            device_id=partner,
            device_id_type=MESH,
        ).wait()
        gi_sum[...] = jnp.sum(gi_in[...].astype(F32), axis=0)

        gy_box[...] = jnp.zeros_like(gy_box)
        for yy in range(2 * NYL):
            for core in range(2):
                q = (yy // NYL) * 2 + core
                r = (yy % NYL) * half
                gy_box[yy * 2 + core, 0:half, 0:HD] = gi_sum[
                    r : r + half, q * HD : (q + 1) * HD
                ].astype(BF16)

        def gy_copy(yy, core):
            return pltpu.make_async_remote_copy(
                src_ref=gy_box.at[yy * 2 + core],
                dst_ref=gy_in.at[c * 2 * NYL + y],
                send_sem=gy_send,
                recv_sem=gy_recv,
                device_id=(z * NYL + yy % NYL, ((yy // NYL) * NX + x) * 2 + core),
                device_id_type=MESH,
            )

        gy_copy(y, other).start()

        @pl.loop(1, 2 * NYL)
        def _(i):
            yy = lax.rem(y + i, 2 * NYL)
            gy_copy(yy, 0).start()
            gy_copy(yy, 1).start()

        gy_in[c * 2 * NYL + y] = gy_box[y * 2 + c]

        pltpu.make_async_remote_copy(
            src_ref=gtz_in.at[pl.ds(0, nz - 1)],
            dst_ref=gtz_in.at[pl.ds(0, nz - 1)],
            send_sem=gtz_send,
            recv_sem=gtz_recv,
            device_id=partner,
            device_id_type=MESH,
        ).wait()
        summed = jnp.sum(gtz_in[...].astype(F32), axis=0)
        for t in range(texts_here):
            for p in range(pieces):
                r = t * pieces + p
                grad_text[t : t + 1, p * LANES : (p + 1) * LANES] = summed[r : r + 1, :]

        pltpu.make_async_remote_copy(
            src_ref=gy_in.at[pl.ds(0, 4 * NYL - 1)],
            dst_ref=gy_in.at[pl.ds(0, 4 * NYL - 1)],
            send_sem=gy_send,
            recv_sem=gy_recv,
            device_id=partner,
            device_id_type=MESH,
        ).wait()
        for core in range(2):
            part = gy_in[core * 2 * NYL : (core + 1) * 2 * NYL].astype(F32)
            grad_image[core * half : (core + 1) * half, :] = jnp.sum(part, axis=0)[0:half, 0:HD]

        @pl.when(my_half == c)
        def _():
            pltpu.make_async_remote_copy(
                src_ref=outbox.at[pl.ds(0, dp_size - 1)],
                dst_ref=outbox.at[pl.ds(0, dp_size - 1)],
                send_sem=a2a_send,
                recv_sem=a2a_recv,
                device_id=partner,
                device_id_type=MESH,
            ).wait_send()

        @pl.when(my_half != c)
        def _():
            pltpu.make_async_remote_copy(
                src_ref=outbox,
                dst_ref=outbox,
                send_sem=a2a_send,
                recv_sem=a2a_recv,
                device_id=partner,
                device_id_type=MESH,
            ).wait_send()

        for k in range(images_here):
            pltpu.make_async_remote_copy(
                src_ref=feats.at[k, pl.ds(0, NG - 1)],
                dst_ref=feats.at[k, pl.ds(0, NG - 1)],
                send_sem=g_send.at[k],
                recv_sem=g_recv.at[k, 0],
                device_id=partner,
                device_id_type=MESH,
            ).wait_send()

    dma = pltpu.SemaphoreType.DMA
    scratch = [
        pltpu.VMEM((dp_size, MAXP, HD), BF16),
        pltpu.VMEM((2 * half, MAXP, HD), BF16),
        pltpu.VMEM((3 * HD, width), BF16),
        pltpu.VMEM((HD, width), BF16),
        pltpu.VMEM((images_here, NG, 2 * HD, LANES), BF16),
        pltpu.VMEM((packed, LANES), F32),
        pltpu.VMEM((packed, LANES), BF16),
        pltpu.VMEM((2 * nz, packed, LANES), BF16),
        pltpu.VMEM((2 * nz * packed, LANES), F32),
        pltpu.VMEM((text_rows, width), F32),
        pltpu.VMEM((text_rows, NX * wide), F32),
        pltpu.VMEM((NG * packed, LANES), F32),
        pltpu.VMEM((NG, packed, LANES), BF16),
        pltpu.VMEM((NG, packed, LANES), BF16),
        pltpu.VMEM((packed, LANES), F32),
        pltpu.VMEM((packed, LANES), BF16),
        pltpu.VMEM((plane, packed, LANES), BF16),
        pltpu.VMEM((plane * packed, LANES), F32),
        pltpu.VMEM((rows, width), F32),
        pltpu.VMEM((NX, rows, wide), BF16),
        pltpu.VMEM((NX, rows, wide), BF16),
        pltpu.VMEM((rows, wide), F32),
        pltpu.VMEM((4 * NYL, -(-half // 16) * 16, LANES), BF16),
        pltpu.VMEM((4 * NYL, -(-half // 16) * 16, LANES), BF16),
        pltpu.VMEM((2 * nz * packed, LANES), F32),
        pltpu.VMEM((nz * packed, LANES), F32),
        pltpu.VMEM((nz, packed, LANES), BF16),
        pltpu.VMEM((nz, packed, LANES), BF16),
        dma,
        dma,
        dma,
        dma((2,)),
        dma((2,)),
        dma((images_here,)),
        dma((images_here, NG)),
        dma,
        dma,
        dma,
        dma,
        dma,
        dma,
        dma,
        dma,
        dma,
        dma,
        dma,
        dma,
        dma,
        dma,
    ]
    return kernel, scratch


def on_device(patches, counts, dest, w_qkv, w_out, text):
    dp_size = lax.axis_size("dp")
    width = w_qkv.shape[2]
    texts_here = text.shape[0]
    kernel, scratch = make_kernel(dp_size, width, texts_here)
    vmem = pl.BlockSpec(memory_space=pltpu.VMEM)
    return pl.pallas_call(
        kernel,
        out_shape=(
            jax.ShapeDtypeStruct((dp_size, HD), F32),
            jax.ShapeDtypeStruct((texts_here, width), F32),
        ),
        in_specs=[vmem] * 6,
        out_specs=(vmem, vmem),
        scratch_shapes=scratch,
        compiler_params=pltpu.CompilerParams(
            collective_id=0, has_side_effects=True, vmem_limit_bytes=40 * 1024 * 1024
        ),
    )(
        counts.reshape(dp_size, dp_size),
        dest.reshape(dp_size, dp_size),
        patches,
        w_qkv.reshape(3 * HD, width),
        w_out,
        text,
    )


def solution(mesh):
    placed = (P("mp", "dp"), P(), P(), P(None, "mp", None), P("mp", None), P(("dp", "mp"), None))
    return jax.shard_map(
        on_device,
        mesh=mesh,
        in_specs=placed,
        out_specs=(P("dp", "mp"), P(("dp", "mp"), None)),
        check_vma=False,
    )
```

time: 1100 us -> 92 us (0.08)
  waiting for transfers between devices: 772 us -> 0 us
  starting transfers between devices: 184 us -> 0 us
  Pallas kernels: 0 us -> 85.5 us
  blocking collectives: 31.3 us -> 0 us
  local copies, waits for them, and re-layouts: 36.8 us -> 5.54 us
  matrix products: 29.7 us -> 0 us
  other arithmetic: 23.2 us -> 0 us
  between operations: 14.8 us -> 0.66 us
    ppermute x96 -> x0, waiting for transfers between devices: 299 us -> none  [from_behind(): lax.ppermute(shard, axis, [(i, (i + by) % peers) for i in range(peers)])]
    unnamed x4 -> x0, waiting for transfers between devices: 234 us -> none
    ppermute x96 -> x0, starting transfers between devices: 184 us -> none  [from_behind(): lax.ppermute(shard, axis, [(i, (i + by) % peers) for i in range(peers)])]
    psum x1 -> x0, waiting for transfers between devices: 181 us -> none  [on_device(): pooled = lax.psum(pool_term, 'mp')]
    pallas_call x0 -> x1, Pallas kernels: none -> 85.5 us  [on_device(): pl.pallas_call(kernel, out_shape=(jax.ShapeDtypeStruct((dp_size, HD), F32...]
    all_gather x1 -> x0, waiting for transfers between devices: 58.1 us -> none  [on_device(): gathered = lax.all_gather(received, 'mp', axis=1, tiled=True)]
    all_to_all x1 -> x0, blocking collectives: 31.3 us -> none  [on_device(): lax.all_to_all(outgoing, 'dp', split_axis=0, concat_axis=0, tiled=True)]
    dot_general x152 -> x0, matrix products: 29.7 us -> none  [the longest x48 11.8 us: pair_turn(): jnp.einsum('aj,jd->ad', dscaled, travelling_bf, preferred_element_type=jn...]
  transfers between devices with their start and end apart: 99 -> 0, of which waited for: 99 -> 0; matrix products, arithmetic and copies ran while one was open for 3% -> 0% of each run, Pallas kernels for 0% -> 0%
where the time goes in v1:
time: 92 us; the launch traced here: 91.7 us
  Pallas kernels  85.5 us (93%)
  local copies, waits for them, and re-layouts  5.54 us (6%)
    pallas_call x1, Pallas kernels, on_device(): pl.pallas_call(kernel, out_shape=(jax.ShapeDtypeStruct((dp_size, HD), F32...  85.5 us
    unnamed x12, local copies, waits for them, and re-layouts  4.68 us

profile of v1, /device:TPU:1, one launch (start us, length us, event | category | flops | bytes accessed | tf_op | source)
XLA Modules:
  0.0 91.7 jit_solution(4646998123477020682)
XLA Ops:
  0.6 0.0 copy-start.4
  0.6 0.8 reshape.13.counts
  1.4 0.0 copy-done.4
  1.4 0.0 copy-start.3
  1.4 0.1 reshape.14.dest
  1.5 0.6 copy-done.3
  2.1 0.0 copy-start
  2.1 1.0 %copy-done = bf16[3,72,1152]{2,1,0:T(8,128)(2,1)S(1)} copy-done((bf16[3,72,1152]{2,1,0:T(8,128)(2,1)S(1)}, bf16[3,72,1152]{2,1,0:T(8,128)(2,1)}, u32[]{:S(2)}) %copy-start) | copy-done | bytes 497688
  3.2 0.0 copy-start.1
  3.2 0.9 copy-done.1
  4.1 0.0 copy-start.2
  4.1 0.9 copy-done.2
  5.0 85.5 %shard_map.77 = (f32[48,72]{1,0:T(8,128)S(1)}, f32[3,1152]{1,0:T(4,128)S(1)}) custom-call(s32[48,48]{1,0:T(8,128)S(1)} %reshape.13.counts, s32[48,48]{1,0:T(8,128)S(1)} %reshape.14.dest, bf16[72,768]{1,0:T(8,128)(2,1)S(1)} %copy-done.2, bf16[216,1152]{1,0:T(8,128)(2,1)S(1)} %bitcast.1, bf16[72,1152]{1,0:T(8,128)(2,1)S(1)} %copy-done.1, ...), custom_call_target="tpu_custom_call" | custom-call | tf_op jit(solution)/shard_map/pallas_call | solution.py:693
  90.5 0.6 copy.10
  91.1 0.6 copy.11
Async XLA Ops:
  0.6 0.8 copy-start.4
  1.4 0.7 copy-start.3
  2.1 1.0 %copy-start = (bf16[3,72,1152]{2,1,0:T(8,128)(2,1)S(1)}, bf16[3,72,1152]{2,1,0:T(8,128)(2,1)}, u32[]{:S(2)}) copy-start(bf16[3,72,1152]{2,1,0:T(8,128)(2,1)} %param.9) | copy-start | bytes 1492996
  3.2 0.9 copy-start.1
  4.1 0.9 copy-start.2

commit v2 on v1

--- a/solution.py
+++ b/solution.py
@@ -46,19 +46,27 @@
     wide = -(-(4 * HD) // LANES) * LANES
 
     def kernel(
+        counts_in,
+        dest_in,
+        patches_in,
+        w_qkv_in,
+        w_out_in,
+        text_arg,
+        grad_image,
+        grad_text,
         counts,
         dest,
         patches,
         w_qkv,
         w_out,
         text,
-        grad_image,
-        grad_text,
+        in_sem,
         outbox,
         inbox,
         w_qkv_peer,
         w_out_peer,
         feats,
+        qkv,
         text_f,
         text_box,
         text_in,
@@ -116,6 +124,22 @@
         my_slot = me % half
         extra = jnp.where(my_half == c, 0, 1)
 
+        loads = [
+            pltpu.make_async_copy(src, dst, in_sem.at[i])
+            for i, (src, dst) in enumerate(
+                (
+                    (dest_in, dest),
+                    (counts_in, counts),
+                    (patches_in, patches),
+                    (w_qkv_in, w_qkv),
+                    (w_out_in, w_out),
+                    (text_arg, text),
+                )
+            )
+        ]
+        for load in loads:
+            load.start()
+
         barrier = pltpu.get_barrier_semaphore()
 
         def greet(device):
@@ -150,16 +174,34 @@
             q = lax.rem(y + i, 2 * NYL)
             greet((z * NYL + q % NYL, ((q // NYL) * NX + x) * 2 + other))
 
-        own_counts = counts[pl.ds(me, 1), :]
-        own_dest = dest[pl.ds(me, 1), :]
-        lane = iota((slots, dp_size), 1)
-        target = iota((slots, dp_size), 0) // MAXP
-        index = jnp.sum(jnp.where(own_dest == target, lane, 0), axis=1, keepdims=True)
-        start = jnp.sum(jnp.where(lane < index, own_counts, 0), axis=1, keepdims=True)
-        count = jnp.sum(jnp.where(lane == index, own_counts, 0), axis=1, keepdims=True)
-        position = iota((slots, 1), 0) % MAXP
-        column = jnp.where(position < count, start + position, -1)
+        loads[0].wait()
+        loads[1].wait()
+        first = me * dp_size
+        table_rows = dp_size * dp_size // LANES
+        span = iota((dp_size, LANES), 1)
+        target = iota((dp_size, LANES), 0)
+        index = jnp.zeros((dp_size, 1), jnp.int32)
+        base = first // LANES
+        own_rows = []
+        for r in range(2):
+            row = jnp.minimum(base + r, table_rows - 1)
+            image = (base + r) * LANES + span - first
+            inside = (image >= 0) & (image < dp_size) & (base + r < table_rows)
+            image = jnp.where(inside, image, dp_size)
+            own_rows.append((image, counts[pl.ds(row, 1), :]))
+            hit = inside & (dest[pl.ds(row, 1), :] == target)
+            index = index + jnp.sum(jnp.where(hit, image, 0), axis=1, keepdims=True)
+        start = jnp.zeros((dp_size, 1), jnp.int32)
+        count = jnp.zeros((dp_size, 1), jnp.int32)
+        for image, own in own_rows:
+            start = start + jnp.sum(jnp.where(image < index, own, 0), axis=1, keepdims=True)
+            count = count + jnp.sum(jnp.where(image == index, own, 0), axis=1, keepdims=True)
+        position = iota((dp_size, MAXP, 1), 1)
+        column = jnp.where(
+            position < count.reshape(dp_size, 1, 1), start.reshape(dp_size, 1, 1) + position, -1
+        ).reshape(slots, 1)
         chosen = (iota((slots, patches.shape[1]), 1) == column).astype(F32).astype(BF16)
+        loads[2].wait()
         picked = dot_nt(chosen, patches[...]).astype(BF16)
         outbox[...] = picked.reshape(dp_size, MAXP, HD)
 
@@ -176,9 +218,15 @@
                 device_id_type=MESH,
             )
 
-        @pl.loop(1, dp_size)
-        def _(i):
-            image_copy(lax.rem(me + i, dp_size)).start()
+        @pl.loop(0, nz)
+        def _(j):
+            zz = lax.rem(z + nz // 2 + ((j + 1) // 2) * (1 - 2 * (j % 2)) + nz, nz)
+            for i in range(NYL):
+                d = zz * NYL + lax.rem(ylo + NYL - 1 - i, NYL)
+
+                @pl.when(d != me)
+                def _():
+                    image_copy(d).start()
 
         own_copy = pltpu.make_async_copy(
             outbox.at[me], inbox.at[c * half + my_slot], local_sem
@@ -204,9 +252,12 @@
 
         swap_qkv = swap(w_qkv, w_qkv_peer, 0)
         swap_out = swap(w_out, w_out_peer, 1)
+        loads[3].wait()
         swap_qkv.start()
+        loads[4].wait()
         swap_out.start()
 
+        loads[5].wait()
         text_float = text[...].astype(F32)
         text_unit = text_float * lax.rsqrt(
             jnp.sum(text_float * text_float, axis=1, keepdims=True) + 1e-6
@@ -231,18 +282,14 @@
                 device_id_type=MESH,
             )
 
-        text_copy(z, other).start()
-
-        @pl.loop(1, nz)
-        def _(i):
-            zz = lax.rem(z + i, nz)
-            text_copy(zz, 0).start()
-            text_copy(zz, 1).start()
-
-        mine = pl.ds(pl.multiple_of(half * c, 8), half)
-        got = jnp.sum(
-            jnp.where(dest[mine, :] == me, counts[mine, :], 0), axis=1, keepdims=True
-        )
+        got = jnp.zeros((half, LANES), jnp.int32)
+        slot_row, slot_lane = iota((half, LANES), 0), iota((half, LANES), 1)
+        half_rows = half * dp_size // LANES
+        for r in range(half_rows):
+            row = pl.ds(half_rows * c + r, 1)
+            inside = (r * LANES + slot_lane) // dp_size == slot_row
+            got = got + jnp.where(inside & (dest[row, :] == me), counts[row, :], 0)
+        got = jnp.sum(got, axis=1, keepdims=True)
 
         @pl.when(my_half == c)
         def _():
@@ -295,6 +342,14 @@
             feat_copy(k, g, left).start()
             feat_copy(k, g, right).start()
 
+        text_copy(z, other).start()
+
+        @pl.loop(1, nz)
+        def _(i):
+            zz = lax.rem(z + i, nz)
+            text_copy(zz, 0).start()
+            text_copy(zz, 1).start()
+
         def relay(k, row, flip):
             feat_copy(k, row + left_x, left).wait_recv()
             if not flip:
@@ -314,17 +369,20 @@
 
         part_f[...] = jnp.zeros_like(part_f)
         mean_f[...] = jnp.zeros_like(mean_f)
-        row8, lane8 = iota((NG, LANES), 0), iota((NG, LANES), 1)
-        same = iota((LANES, LANES), 0) // MAXP == iota((LANES, LANES), 1) // MAXP
         for k in range(images_here):
             relay(k, far_row, k % 2 == 0)
             feat_copy(k, own_row + far_x, left).wait_recv()
             feat_copy(k, far_row + far_x, left).wait_recv()
-            raw = feats[k].reshape(width, LANES)
-            full = raw.astype(F32)
+            full = feats[k].reshape(width, LANES).astype(F32)
             centred = full - jnp.sum(full, axis=0, keepdims=True) / width
             variance = jnp.sum(centred * centred, axis=0, keepdims=True) / width
             normed = (centred * lax.rsqrt(variance + 1e-6)).astype(BF16)
+            qkv[k, 0] = dot_nn(w_qkv[...], normed)
+            qkv[k, 1] = dot_nn(w_qkv_peer[...], normed)
+        row8, lane8 = iota((NG, LANES), 0), iota((NG, LANES), 1)
+        same = iota((LANES, LANES), 0) // MAXP == iota((LANES, LANES), 1) // MAXP
+        terms = []
+        for k in range(images_here):
             got_k = got[k * NG : (k + 1) * NG]
             got_float = got_k.astype(F32)
             real = (lane8 // MAXP == row8) & (lane8 % MAXP < got_k)
@@ -333,11 +391,10 @@
             member = real_float.astype(BF16)
             keep = same & key_real
             term = jnp.zeros((NG, width), F32)
-            for wq, wo in ((w_qkv, w_out), (w_qkv_peer, w_out_peer)):
-                projected = dot_nn(wq[...], normed)
-                query = jnp.transpose(projected[0:HD]).astype(BF16)
-                key = projected[HD : 2 * HD].astype(BF16)
-                value = projected[2 * HD : 3 * HD].astype(BF16)
+            for h, wo in enumerate((w_out, w_out_peer)):
+                query = jnp.transpose(qkv[k, h, 0:HD]).astype(BF16)
+                key = qkv[k, h, HD : 2 * HD].astype(BF16)
+                value = qkv[k, h, 2 * HD : 3 * HD].astype(BF16)
                 scores = dot_nn(query, key) / math.sqrt(HD)
                 scores = jnp.where(keep, scores, -1e30)
                 raised = jnp.exp(scores - jnp.max(scores, axis=1, keepdims=True))
@@ -345,18 +402,12 @@
                 mixed = dot_nt(value, weights).astype(BF16)
                 pooled = (dot_nt(member, mixed) / got_float).astype(BF16)
                 term = term + dot_nn(pooled, wo[...])
+            terms.append(term)
+        for k in range(images_here):
             for p in range(pieces):
-                part_f[pl.ds(k * pieces + p, NG, stride=packed), :] = term[
+                part_f[pl.ds(k * pieces + p, NG, stride=packed), :] = terms[k][
                     :, p * LANES : (p + 1) * LANES
                 ]
-            here = (lane8 // MAXP == g).astype(F32).astype(BF16)
-            own_got = jnp.sum(
-                jnp.where(iota((NG, 1), 0) == g, got_float, 0.0), axis=0, keepdims=True
-            )
-            mean = dot_nt(here, raw) / own_got
-            for p in range(pieces):
-                r = k * pieces + p
-                mean_f[r : r + 1, :] = mean[0:1, p * LANES : (p + 1) * LANES]
 
         part_b[...] = part_f[...].astype(BF16).reshape(NG, packed, LANES)
 
@@ -375,6 +426,18 @@
             part_copy(lax.rem(g + i, NG)).start()
 
         part_in[g] = part_b[g]
+
+        here = (lane8 // MAXP == g).astype(F32).astype(BF16)
+        for k in range(images_here):
+            own_got = jnp.sum(
+                jnp.where(iota((NG, 1), 0) == g, got[k * NG : (k + 1) * NG], 0),
+                axis=0,
+                keepdims=True,
+            ).astype(F32)
+            mean = dot_nt(here, feats[k].reshape(width, LANES)) / own_got
+            for p in range(pieces):
+                r = k * pieces + p
+                mean_f[r : r + 1, :] = mean[0:1, p * LANES : (p + 1) * LANES]
 
         pltpu.make_async_remote_copy(
             src_ref=text_in.at[pl.ds(0, 2 * nz - 1)],
@@ -431,9 +494,32 @@
                 device_id_type=MESH,
             )
 
-        @pl.loop(1, plane)
-        def _(i):
-            unit_copy(lax.rem(place + i, plane)).start()
+        @pl.loop(0, 2 * NYL)
+        def _(j):
+            yy = lax.rem(y + NYL + ((j + 1) // 2) * (1 - 2 * (j % 2)) + 2 * NYL, 2 * NYL)
+            for i in (2, 1, 3, 0):
+                q = (yy % NYL) * NG + (yy // NYL) * NX + lax.rem(x + i, NX)
+
+                @pl.when(q != place)
+                def _():
+                    unit_copy(q).start()
+
+        text_row = iota((text_rows, 1), 0)
+        text_source = (text_row % nz) * NYL + ylo
+        text_core = (text_row % (2 * nz)) // nz
+        pair_at = text_source * dp_size + (g * 2 + text_core) * texts_here + text_row // (2 * nz)
+        pair_lane = iota((text_rows, LANES), 1)
+        pair_dest = jnp.zeros((text_rows, LANES), jnp.int32)
+        for r in range(table_rows):
+            pair_dest = pair_dest + jnp.where(
+                pair_at == r * LANES + pair_lane, dest[r : r + 1, :], 0
+            )
+        pair_dest = jnp.sum(pair_dest, axis=1, keepdims=True)
+        image_lane = iota((text_rows, rows), 1)
+        image_source = c * half + image_lane % half
+        image_dest = z * NYL + image_lane // half
+        paired = (image_source == text_source) & (image_dest == pair_dest)
+        labels = jnp.where(paired, 1.0, -1.0)
 
         pltpu.make_async_remote_copy(
             src_ref=unit_in.at[pl.ds(0, plane - 1)],
@@ -455,27 +541,27 @@
                     ]
         units = unit_full[...].astype(BF16)
 
-        text_id = iota((text_rows, dp_size), 0)
-        text_z = text_id % nz
-        text_core = (text_id % (2 * nz)) // nz
-        text_t = text_id // (2 * nz)
-        col = iota((text_rows, dp_size), 1)
-        source = (col == text_z * NYL + ylo).astype(F32).astype(BF16)
-        dest_rows = dot_nn(source, dest[...].astype(F32).astype(BF16))
-        pair_col = (g * 2 + text_core) * texts_here + text_t
-        pair_dest = jnp.sum(
-            jnp.where(col == pair_col, dest_rows, 0.0), axis=1, keepdims=True
-        ).astype(jnp.int32)
-        image_lane = iota((text_rows, rows), 1)
-        image_source = c * half + image_lane % half
-        image_dest = z * NYL + image_lane // half
-        text_source = (iota((text_rows, 1), 0) % nz) * NYL + ylo
-        paired = (image_source == text_source) & (image_dest == pair_dest)
-        labels = jnp.where(paired, 1.0, -1.0)
         logits = 4.0 * dot_nt(text_rows_b, units) - 2.0
         dscaled = -4.0 * labels / (1.0 + jnp.exp(labels * logits))
         turned = jnp.transpose(dscaled).astype(BF16)
         dscaled = dscaled.astype(BF16)
+
+        for xx in range(NX):
+            gi_box[xx] = dot_nn(turned, text_cols_b[:, xx * wide : (xx + 1) * wide]).astype(BF16)
+
+        def gi_copy(xx):
+            return pltpu.make_async_remote_copy(
+                src_ref=gi_box.at[xx],
+                dst_ref=gi_in.at[x],
+                send_sem=gi_send,
+                recv_sem=gi_recv,
+                device_id=(me, (yhi * NX + xx) * 2 + c),
+                device_id_type=MESH,
+            )
+
+        for i in range(1, NX):
+            gi_copy(lax.rem(x + i, NX)).start()
+        gi_in[x] = gi_box[x]
 
         text_grad = dot_nn(dscaled, units)
         gt_f[...] = jnp.zeros_like(gt_f)
@@ -495,26 +581,9 @@
         )
         gt_copy.start()
 
-        for xx in range(NX):
-            gi_box[xx] = dot_nn(turned, text_cols_b[:, xx * wide : (xx + 1) * wide]).astype(BF16)
-
-        def gi_copy(xx):
-            return pltpu.make_async_remote_copy(
-                src_ref=gi_box.at[xx],
-                dst_ref=gi_in.at[x],
-                send_sem=gi_send,
-                recv_sem=gi_recv,
-                device_id=(me, (yhi * NX + xx) * 2 + c),
-                device_id_type=MESH,
-            )
-
-        for i in range(1, NX):
-            gi_copy(lax.rem(x + i, NX)).start()
-        gi_in[x] = gi_box[x]
-
         gt_copy.wait()
-        own_rows = gt_f[pl.ds(pl.multiple_of(c * core_rows, 8), core_rows), :]
-        gt_box[...] = (own_rows + gt_in[...]).astype(BF16).reshape(nz, packed, LANES)
+        own_sums = gt_f[pl.ds(pl.multiple_of(c * core_rows, 8), core_rows), :]
+        gt_box[...] = (own_sums + gt_in[...]).astype(BF16).reshape(nz, packed, LANES)
 
         def gtz_copy(zz):
             return pltpu.make_async_remote_copy(
@@ -631,11 +700,19 @@
 
     dma = pltpu.SemaphoreType.DMA
     scratch = [
+        pltpu.VMEM((dp_size * dp_size // LANES, LANES), jnp.int32),
+        pltpu.VMEM((dp_size * dp_size // LANES, LANES), jnp.int32),
+        pltpu.VMEM((HD, dp_size * MAXP), BF16),
+        pltpu.VMEM((3 * HD, width), BF16),
+        pltpu.VMEM((HD, width), BF16),
+        pltpu.VMEM((texts_here, width), BF16),
+        dma((6,)),
         pltpu.VMEM((dp_size, MAXP, HD), BF16),
         pltpu.VMEM((2 * half, MAXP, HD), BF16),
         pltpu.VMEM((3 * HD, width), BF16),
         pltpu.VMEM((HD, width), BF16),
         pltpu.VMEM((images_here, NG, 2 * HD, LANES), BF16),
+        pltpu.VMEM((images_here, 2, 3 * HD, LANES), F32),
         pltpu.VMEM((packed, LANES), F32),
         pltpu.VMEM((packed, LANES), BF16),
         pltpu.VMEM((2 * nz, packed, LANES), BF16),
@@ -696,15 +773,15 @@
             jax.ShapeDtypeStruct((dp_size, HD), F32),
             jax.ShapeDtypeStruct((texts_here, width), F32),
         ),
-        in_specs=[vmem] * 6,
+        in_specs=[pl.BlockSpec(memory_space=pltpu.HBM)] * 6,
         out_specs=(vmem, vmem),
         scratch_shapes=scratch,
         compiler_params=pltpu.CompilerParams(
             collective_id=0, has_side_effects=True, vmem_limit_bytes=40 * 1024 * 1024
         ),
     )(
-        counts.reshape(dp_size, dp_size),
-        dest.reshape(dp_size, dp_size),
+        counts.reshape(-1, LANES),
+        dest.reshape(-1, LANES),
         patches,
         w_qkv.reshape(3 * HD, width),
         w_out,

time: 92 us -> 89 us (0.967)
  Pallas kernels: 85.5 us -> 81.8 us
    pallas_call x1, Pallas kernels: 85.5 us -> 81.8 us  [on_device(): pl.pallas_call(kernel, out_shape=(jax.ShapeDtypeStruct((dp_size, HD), F32...]
    unnamed x12 -> x14, local copies, waits for them, and re-layouts: 4.68 us -> 6.16 us
where the time goes in v2:
time: 89 us; the launch traced here: 88.6 us
  Pallas kernels  81.8 us (92%)
  local copies, waits for them, and re-layouts  6.16 us (7%)
    pallas_call x1, Pallas kernels, on_device(): pl.pallas_call(kernel, out_shape=(jax.ShapeDtypeStruct((dp_size, HD), F32...  81.8 us
    unnamed x14, local copies, waits for them, and re-layouts  6.16 us

profile of v2, /device:TPU:1, one launch (start us, length us, event | category | flops | bytes accessed | tf_op | source)
XLA Modules:
  0.0 88.6 jit_solution(17587957805797801961)
XLA Ops:
  0.6 0.0 copy-start
  0.6 1.0 %copy-done = bf16[3,72,1152]{2,1,0:T(8,128)(2,1)S(1)} copy-done((bf16[3,72,1152]{2,1,0:T(8,128)(2,1)S(1)}, bf16[3,72,1152]{2,1,0:T(8,128)(2,1)}, u32[]{:S(2)}) %copy-start) | copy-done | bytes 497688
  1.7 0.0 copy-start.1
  1.7 0.9 %copy-done.1 = bf16[72,1152]{1,0:T(8,128)(2,1)S(1)} copy-done((bf16[72,1152]{1,0:T(8,128)(2,1)S(1)}, bf16[72,1152]{1,0:T(8,128)(2,1)}, u32[]{:S(2)}) %copy-start.1) | copy-done | bytes 165912
  2.6 0.0 copy-start.2
  2.6 0.9 %copy-done.2 = bf16[72,768]{1,0:T(8,128)(2,1)S(1)} copy-done((bf16[72,768]{1,0:T(8,128)(2,1)S(1)}, bf16[72,768]{1,0:T(8,128)(2,1)}, u32[]{:S(2)}) %copy-start.2) | copy-done | bytes 110616
  3.5 0.0 copy-start.3
  3.5 0.7 copy-done.3
  4.2 0.0 copy-start.4
  4.2 0.7 copy-done.4
  4.9 0.0 copy-start.5
  4.9 0.7 copy-done.5
  5.6 81.8 %shard_map.77 = (f32[48,72]{1,0:T(8,128)S(1)}, f32[3,1152]{1,0:T(4,128)S(1)}) custom-call(s32[18,128]{1,0:T(8,128)S(1)} %bitcast.4, s32[18,128]{1,0:T(8,128)S(1)} %bitcast.5, bf16[72,768]{1,0:T(8,128)(2,1)S(1)} %copy-done.2, bf16[216,1152]{1,0:T(8,128)(2,1)S(1)} %bitcast.3, bf16[72,1152]{1,0:T(8,128)(2,1)S(1)} %copy-done.1, bf16[3,1152]{1,0:T(4,128)(2,1)S(1)} %copy-done.5), custom_call_target="tpu_custom_call" | custom-call | tf_op jit(solution)/shard_map/pallas_call | solution.py:770
  87.4 0.6 copy.10
  88.0 0.6 copy.11
Async XLA Ops:
  0.6 1.0 %copy-start = (bf16[3,72,1152]{2,1,0:T(8,128)(2,1)S(1)}, bf16[3,72,1152]{2,1,0:T(8,128)(2,1)}, u32[]{:S(2)}) copy-start(bf16[3,72,1152]{2,1,0:T(8,128)(2,1)} %param.9) | copy-start | bytes 1492996
  1.7 0.9 %copy-start.1 = (bf16[72,1152]{1,0:T(8,128)(2,1)S(1)}, bf16[72,1152]{1,0:T(8,128)(2,1)}, u32[]{:S(2)}) copy-start(bf16[72,1152]{1,0:T(8,128)(2,1)} %w_out_in.1) | copy-start | bytes 497668
  2.6 0.9 %copy-start.2 = (bf16[72,768]{1,0:T(8,128)(2,1)S(1)}, bf16[72,768]{1,0:T(8,128)(2,1)}, u32[]{:S(2)}) copy-start(bf16[72,768]{1,0:T(8,128)(2,1)} %patches_in.1) | copy-start | bytes 331780
  3.5 0.7 copy-start.3
  4.2 0.7 copy-start.4
  4.9 0.7 copy-start.5

commit v3 on v2

--- a/solution.py
+++ b/solution.py
@@ -29,6 +29,10 @@
 
 def dot_nt(a, b):
     return lax.dot_general(a, b, (((1,), (1,)), ((), ())), preferred_element_type=F32)
+
+
+def wrap(value, size):
+    return jnp.where(value >= size, value - size, value)
 
 
 def make_kernel(dp_size, width, texts_here):
@@ -99,6 +103,8 @@
         g_recv,
         text_send,
         text_recv,
+        swap_send,
+        swap_recv,
         part_send,
         part_recv,
         unit_send,
@@ -158,21 +164,22 @@
 
         @pl.loop(1, nz)
         def _(i):
-            zz = lax.rem(z + i, nz)
-            greet((zz * NYL + ylo, g * 2))
-            greet((zz * NYL + ylo, g * 2 + 1))
+            greet((wrap(z + i, nz) * NYL + ylo, mp))
 
         place = ylo * NG + g
 
         @pl.loop(1, plane)
         def _(i):
-            q = lax.rem(place + i, plane)
+            q = (place + i) % plane
             greet((z * NYL + q // NG, (q % NG) * 2 + c))
 
         @pl.loop(1, 2 * NYL)
         def _(i):
-            q = lax.rem(y + i, 2 * NYL)
+            q = (y + i) % (2 * NYL)
             greet((z * NYL + q % NYL, ((q // NYL) * NX + x) * 2 + other))
+
+        for buffer in (text_f, text_pad, part_f, mean_f, gt_f, gy_box):
+            buffer[...] = jnp.zeros_like(buffer)
 
         loads[0].wait()
         loads[1].wait()
@@ -205,7 +212,7 @@
         picked = dot_nt(chosen, patches[...]).astype(BF16)
         outbox[...] = picked.reshape(dp_size, MAXP, HD)
 
-        total = (2 * half - 1 + extra) + 1 + 2 * (nz - 1) + (plane - 1) + (2 * NYL - 1)
+        total = (2 * half - 1 + extra) + 1 + (nz - 1) + (plane - 1) + (2 * NYL - 1)
         pl.semaphore_wait(barrier, total)
 
         def image_copy(d):
@@ -220,9 +227,11 @@
 
         @pl.loop(0, nz)
         def _(j):
-            zz = lax.rem(z + nz // 2 + ((j + 1) // 2) * (1 - 2 * (j % 2)) + nz, nz)
+            step = (j + 1) // 2
+            zz = wrap(z + nz // 2 + jnp.where(j % 2 == 1, nz - step, step), nz)
+            zz = wrap(zz, nz)
             for i in range(NYL):
-                d = zz * NYL + lax.rem(ylo + NYL - 1 - i, NYL)
+                d = zz * NYL + (ylo + NYL - 1 - i) % NYL
 
                 @pl.when(d != me)
                 def _():
@@ -262,7 +271,6 @@
         text_unit = text_float * lax.rsqrt(
             jnp.sum(text_float * text_float, axis=1, keepdims=True) + 1e-6
         )
-        text_f[...] = jnp.zeros_like(text_f)
         for t in range(texts_here):
             for k in range(pieces):
                 text_f[t * pieces + k : t * pieces + k + 1, :] = text_unit[
@@ -272,15 +280,25 @@
         text_box[...] = own_text
         text_in[c * nz + z] = own_text
 
-        def text_copy(zz, core):
+        def text_copy(zz):
             return pltpu.make_async_remote_copy(
                 src_ref=text_box,
                 dst_ref=text_in.at[c * nz + z],
                 send_sem=text_send,
                 recv_sem=text_recv,
-                device_id=(zz * NYL + ylo, g * 2 + core),
-                device_id_type=MESH,
-            )
+                device_id=(zz * NYL + ylo, mp),
+                device_id_type=MESH,
+            )
+
+        own_texts = text_in.at[pl.ds(c * nz, nz)]
+        text_swap = pltpu.make_async_remote_copy(
+            src_ref=own_texts,
+            dst_ref=own_texts,
+            send_sem=swap_send,
+            recv_sem=swap_recv,
+            device_id=partner,
+            device_id_type=MESH,
+        )
 
         got = jnp.zeros((half, LANES), jnp.int32)
         slot_row, slot_lane = iota((half, LANES), 0), iota((half, LANES), 1)
@@ -342,43 +360,44 @@
             feat_copy(k, g, left).start()
             feat_copy(k, g, right).start()
 
-        text_copy(z, other).start()
-
         @pl.loop(1, nz)
         def _(i):
-            zz = lax.rem(z + i, nz)
-            text_copy(zz, 0).start()
-            text_copy(zz, 1).start()
-
-        def relay(k, row, flip):
-            feat_copy(k, row + left_x, left).wait_recv()
-            if not flip:
-                feat_copy(k, row + left_x, right).start()
-            feat_copy(k, row + right_x, left).wait_recv()
-            if flip:
-                feat_copy(k, row + right_x, left).start()
+            text_copy(wrap(z + i, nz)).start()
 
         for k in range(images_here):
-            relay(k, own_row, k % 2 == 1)
+            feat_copy(k, left, left).wait_recv()
+            if k % 2 == 0:
+                feat_copy(k, left, right).start()
+            feat_copy(k, right, left).wait_recv()
+            if k % 2 == 1:
+                feat_copy(k, right, left).start()
             feat_copy(k, across, across).wait_recv()
+            feat_copy(k, across, own_row + far_x).start()
             feat_copy(k, across, left).start()
             feat_copy(k, across, right).start()
 
         swap_qkv.wait()
         swap_out.wait()
 
-        part_f[...] = jnp.zeros_like(part_f)
-        mean_f[...] = jnp.zeros_like(mean_f)
         for k in range(images_here):
-            relay(k, far_row, k % 2 == 0)
             feat_copy(k, own_row + far_x, left).wait_recv()
-            feat_copy(k, far_row + far_x, left).wait_recv()
+            for xx in (left_x, right_x, far_x):
+                feat_copy(k, far_row + xx, left).wait_recv()
             full = feats[k].reshape(width, LANES).astype(F32)
             centred = full - jnp.sum(full, axis=0, keepdims=True) / width
             variance = jnp.sum(centred * centred, axis=0, keepdims=True) / width
             normed = (centred * lax.rsqrt(variance + 1e-6)).astype(BF16)
             qkv[k, 0] = dot_nn(w_qkv[...], normed)
             qkv[k, 1] = dot_nn(w_qkv_peer[...], normed)
+        pltpu.make_async_remote_copy(
+            src_ref=text_in.at[pl.ds(0, nz - 1)],
+            dst_ref=text_in.at[pl.ds(0, nz - 1)],
+            send_sem=text_send,
+            recv_sem=text_recv,
+            device_id=partner,
+            device_id_type=MESH,
+        ).wait()
+        text_swap.start()
         row8, lane8 = iota((NG, LANES), 0), iota((NG, LANES), 1)
         same = iota((LANES, LANES), 0) // MAXP == iota((LANES, LANES), 1) // MAXP
         terms = []
@@ -423,7 +442,7 @@
 
         @pl.loop(1, NG)
         def _(i):
-            part_copy(lax.rem(g + i, NG)).start()
+            part_copy((g + i) % NG).start()
 
         part_in[g] = part_b[g]
 
@@ -439,21 +458,13 @@
                 r = k * pieces + p
                 mean_f[r : r + 1, :] = mean[0:1, p * LANES : (p + 1) * LANES]
 
-        pltpu.make_async_remote_copy(
-            src_ref=text_in.at[pl.ds(0, 2 * nz - 1)],
-            dst_ref=text_in.at[pl.ds(0, 2 * nz - 1)],
-            send_sem=text_send,
-            recv_sem=text_recv,
-            device_id=partner,
-            device_id_type=MESH,
-        ).wait()
+        text_swap.wait()
         text_wide[...] = text_in[...].astype(F32).reshape(2 * nz * packed, LANES)
         for t in range(texts_here):
             for p in range(pieces):
                 text_full[t * 2 * nz : (t + 1) * 2 * nz, p * LANES : (p + 1) * LANES] = (
                     text_wide[pl.ds(t * pieces + p, 2 * nz, stride=packed), :]
                 )
-        text_pad[...] = jnp.zeros_like(text_pad)
         for xx in range(NX):
             for q in range(4):
                 m = ((q // 2) * NX + xx) * 2 + q % 2
@@ -496,9 +507,10 @@
 
         @pl.loop(0, 2 * NYL)
         def _(j):
-            yy = lax.rem(y + NYL + ((j + 1) // 2) * (1 - 2 * (j % 2)) + 2 * NYL, 2 * NYL)
+            step = (j + 1) // 2
+            yy = (y + NYL + jnp.where(j % 2 == 1, 2 * NYL - step, step)) % (2 * NYL)
             for i in (2, 1, 3, 0):
-                q = (yy % NYL) * NG + (yy // NYL) * NX + lax.rem(x + i, NX)
+                q = (yy % NYL) * NG + (yy // NYL) * NX + (x + i) % NX
 
                 @pl.when(q != place)
                 def _():
@@ -564,7 +576,6 @@
         gi_in[x] = gi_box[x]
 
         text_grad = dot_nn(dscaled, units)
-        gt_f[...] = jnp.zeros_like(gt_f)
         for t in range(texts_here):
             for p in range(pieces):
                 gt_f[pl.ds(t * pieces + p, 2 * nz, stride=packed), :] = text_grad[
@@ -597,7 +608,7 @@
 
         @pl.loop(1, nz)
         def _(i):
-            gtz_copy(lax.rem(z + i, nz)).start()
+            gtz_copy(wrap(z + i, nz)).start()
 
         gtz_in[z] = gt_box[z]
 
@@ -611,7 +622,6 @@
         ).wait()
         gi_sum[...] = jnp.sum(gi_in[...].astype(F32), axis=0)
 
-        gy_box[...] = jnp.zeros_like(gy_box)
         for yy in range(2 * NYL):
             for core in range(2):
                 q = (yy // NYL) * 2 + core
@@ -634,7 +644,7 @@
 
         @pl.loop(1, 2 * NYL)
         def _(i):
-            yy = lax.rem(y + i, 2 * NYL)
+            yy = (y + i) % (2 * NYL)
             gy_copy(yy, 0).start()
             gy_copy(yy, 1).start()
 
@@ -757,6 +767,8 @@
         dma,
         dma,
         dma,
+        dma,
+        dma,
     ]
     return kernel, scratch
 
@@ -777,7 +789,7 @@
         out_specs=(vmem, vmem),
         scratch_shapes=scratch,
         compiler_params=pltpu.CompilerParams(
-            collective_id=0, has_side_effects=True, vmem_limit_bytes=40 * 1024 * 1024
+            collective_id=0, has_side_effects=True, vmem_limit_bytes=58 * 1024 * 1024
         ),
     )(
         counts.reshape(-1, LANES),

time: 89 us -> 77.8 us (0.87)
  Pallas kernels: 81.8 us -> 75 us
  local copies, waits for them, and re-layouts: 6.16 us -> 1.96 us
    pallas_call x1, Pallas kernels: 81.8 us -> 75 us  [on_device(): pl.pallas_call(kernel, out_shape=(jax.ShapeDtypeStruct((dp_size, HD), F32...]
    unnamed x14 -> x4, local copies, waits for them, and re-layouts: 6.16 us -> 1.96 us
where the time goes in v3:
time: 77.8 us; the launch traced here: 77.6 us
  Pallas kernels  75 us (96%)
  local copies, waits for them, and re-layouts  1.96 us (3%)
    pallas_call x1, Pallas kernels, on_device(): pl.pallas_call(kernel, out_shape=(jax.ShapeDtypeStruct((dp_size, HD), F32...  75 us
    unnamed x4, local copies, waits for them, and re-layouts  1.96 us

profile of v3, /device:TPU:1, one launch (start us, length us, event | category | flops | bytes accessed | tf_op | source)
XLA Modules:
  0.0 77.6 jit_solution(2950034387962066481)
XLA Ops:
  0.6 75.0 %shard_map.77 = (f32[48,72]{1,0:T(8,128)}, f32[3,1152]{1,0:T(4,128)}) custom-call(s32[18,128]{1,0:T(8,128)} %bitcast.4, s32[18,128]{1,0:T(8,128)} %bitcast.5, bf16[72,768]{1,0:T(8,128)(2,1)} %patches_in.1, bf16[216,1152]{1,0:T(8,128)(2,1)} %bitcast.3, bf16[72,1152]{1,0:T(8,128)(2,1)} %w_out_in.1, bf16[3,1152]{1,0:T(4,128)(2,1)} %text_arg.1), custom_call_target="tpu_custom_call" | custom-call | tf_op jit(solution)/shard_map/pallas_call | solution.py:782
  75.7 0.0 copy-start
  75.7 1.4 %copy.10 = f32[48,72]{1,0:T(8,128)} copy(f32[48,72]{1,0:T(8,128)} %get-tuple-element.4) | data formatting | bytes 27648
  77.0 0.0 copy-done
  77.0 0.6 copy.11
Async XLA Ops:
  75.7 1.4 %copy-start = (f32[3,1152]{1,0:T(4,128)S(1)}, f32[3,1152]{1,0:T(4,128)}, u32[]{:S(2)}) copy-start(f32[3,1152]{1,0:T(4,128)} %get-tuple-element.5) | copy-start | bytes 41476

commit v4 on v3

--- a/solution.py
+++ b/solution.py
@@ -81,7 +81,6 @@
         part_b,
         part_in,
         mean_f,
-        unit_box,
         unit_in,
         unit_wide,
         unit_full,
@@ -168,15 +167,15 @@
 
         place = ylo * NG + g
 
-        @pl.loop(1, plane)
-        def _(i):
-            q = (place + i) % plane
-            greet((z * NYL + q // NG, (q % NG) * 2 + c))
-
         @pl.loop(1, 2 * NYL)
         def _(i):
             q = (y + i) % (2 * NYL)
-            greet((z * NYL + q % NYL, ((q // NYL) * NX + x) * 2 + other))
+            greet((z * NYL + q % NYL, ((q // NYL) * NX + x) * 2))
+            greet((z * NYL + q % NYL, ((q // NYL) * NX + x) * 2 + 1))
+
+        for i in range(1, NX):
+            greet((me, (yhi * NX + (x + i) % NX) * 2 + c))
+            greet((me, ((1 - yhi) * NX + (x + i) % NX) * 2 + c))
 
         for buffer in (text_f, text_pad, part_f, mean_f, gt_f, gy_box):
             buffer[...] = jnp.zeros_like(buffer)
@@ -186,7 +185,10 @@
         first = me * dp_size
         table_rows = dp_size * dp_size // LANES
         span = iota((dp_size, LANES), 1)
-        target = iota((dp_size, LANES), 0)
+        order = iota((dp_size, LANES), 0)
+        step = (order // NYL + 1) // 2
+        target = wrap(z + nz // 2 + jnp.where(order // NYL % 2 == 1, nz - step, step), nz)
+        target = wrap(target, nz) * NYL + (ylo + NYL - 1 - order % NYL) % NYL
         index = jnp.zeros((dp_size, 1), jnp.int32)
         base = first // LANES
         own_rows = []
@@ -207,17 +209,11 @@
         column = jnp.where(
             position < count.reshape(dp_size, 1, 1), start.reshape(dp_size, 1, 1) + position, -1
         ).reshape(slots, 1)
-        chosen = (iota((slots, patches.shape[1]), 1) == column).astype(F32).astype(BF16)
         loads[2].wait()
-        picked = dot_nt(chosen, patches[...]).astype(BF16)
-        outbox[...] = picked.reshape(dp_size, MAXP, HD)
-
-        total = (2 * half - 1 + extra) + 1 + (nz - 1) + (plane - 1) + (2 * NYL - 1)
-        pl.semaphore_wait(barrier, total)
-
-        def image_copy(d):
+
+        def image_copy(at, d):
             return pltpu.make_async_remote_copy(
-                src_ref=outbox.at[d],
+                src_ref=outbox.at[at],
                 dst_ref=inbox.at[c * half + my_slot],
                 send_sem=a2a_send,
                 recv_sem=a2a_recv,
@@ -225,20 +221,39 @@
                 device_id_type=MESH,
             )
 
-        @pl.loop(0, nz)
-        def _(j):
-            step = (j + 1) // 2
-            zz = wrap(z + nz // 2 + jnp.where(j % 2 == 1, nz - step, step), nz)
-            zz = wrap(zz, nz)
-            for i in range(NYL):
-                d = zz * NYL + (ylo + NYL - 1 - i) % NYL
-
-                @pl.when(d != me)
-                def _():
-                    image_copy(d).start()
+        total = (2 * half - 1 + extra) + 1 + (nz - 1) + 2 * (2 * NYL - 1) + 2 * (NX - 1)
+        blocks = 4
+        block_rows = slots // blocks
+        block_images = dp_size // blocks
+        block_z = nz // blocks
+        for n in range(blocks):
+            chosen = iota((block_rows, patches.shape[1]), 1) == column[
+                n * block_rows : (n + 1) * block_rows
+            ]
+            picked = dot_nt(chosen.astype(F32).astype(BF16), patches[...]).astype(BF16)
+            outbox[n * block_images : (n + 1) * block_images] = picked.reshape(
+                block_images, MAXP, HD
+            )
+            if n == 0:
+                pl.semaphore_wait(barrier, total)
+            last = n == blocks - 1
+
+            @pl.loop(n * block_z, (n + 1) * block_z - (1 if last else 0))
+            def _(j):
+                step = (j + 1) // 2
+                zz = wrap(z + nz // 2 + jnp.where(j % 2 == 1, nz - step, step), nz)
+                zz = wrap(zz, nz)
+                for i in range(NYL):
+                    d = zz * NYL + (ylo + NYL - 1 - i) % NYL
+                    image_copy(j * NYL + i, d).start()
+
+            if last:
+                for i in range(NYL - 1):
+                    d = z * NYL + (ylo + NYL - 1 - i) % NYL
+                    image_copy((nz - 1) * NYL + i, d).start()
 
         own_copy = pltpu.make_async_copy(
-            outbox.at[me], inbox.at[c * half + my_slot], local_sem
+            outbox.at[dp_size - 1], inbox.at[c * half + my_slot], local_sem
         )
 
         @pl.when(my_half == c)
@@ -247,7 +262,7 @@
 
         @pl.when(my_half != c)
         def _():
-            image_copy(me).start()
+            image_copy(dp_size - 1, me).start()
 
         def swap(src, dst, i):
             return pltpu.make_async_remote_copy(
@@ -333,11 +348,6 @@
             ).wait_recv()
 
         eye = (iota((HD, HD), 0) == iota((HD, HD), 1)).astype(F32).astype(BF16)
-        low = dot_nt(eye, inbox[0:half].reshape(half_slots, HD))
-        high = dot_nt(eye, inbox[half : 2 * half].reshape(half_slots, HD))
-        block = jnp.concatenate([low, high], axis=0).astype(BF16)
-        for k in range(images_here):
-            feats[k, g] = block[:, k * LANES : (k + 1) * LANES]
 
         across = (1 - yhi) * NX + x
         left_x, right_x = lax.rem(x + NX - 1, NX), lax.rem(x + 1, NX)
@@ -356,6 +366,11 @@
         own_row, far_row = yhi * NX, (1 - yhi) * NX
         left, right = own_row + left_x, own_row + right_x
         for k in range(images_here):
+            low, high = (
+                dot_nt(eye, inbox[r + k * NG : r + (k + 1) * NG].reshape(LANES, HD))
+                for r in (0, half)
+            )
+            feats[k, g] = jnp.concatenate([low, high], axis=0).astype(BF16)
             feat_copy(k, g, across).start()
             feat_copy(k, g, left).start()
             feat_copy(k, g, right).start()
@@ -400,32 +415,32 @@
         text_swap.start()
         row8, lane8 = iota((NG, LANES), 0), iota((NG, LANES), 1)
         same = iota((LANES, LANES), 0) // MAXP == iota((LANES, LANES), 1) // MAXP
-        terms = []
+        heads = ([], [])
         for k in range(images_here):
             got_k = got[k * NG : (k + 1) * NG]
             got_float = got_k.astype(F32)
             real = (lane8 // MAXP == row8) & (lane8 % MAXP < got_k)
-            real_float = real.astype(F32)
-            key_real = jnp.max(real_float, axis=0, keepdims=True) > 0.5
-            member = real_float.astype(BF16)
-            keep = same & key_real
-            term = jnp.zeros((NG, width), F32)
-            for h, wo in enumerate((w_out, w_out_peer)):
-                query = jnp.transpose(qkv[k, h, 0:HD]).astype(BF16)
-                key = qkv[k, h, HD : 2 * HD].astype(BF16)
+            member = real.astype(F32).astype(BF16)
+            key_count = jnp.broadcast_to(got_k.reshape(NG, 1, 1), (NG, MAXP, 1))
+            key_count = key_count.reshape(LANES, 1)
+            keep = same & (iota((LANES, 1), 0) % MAXP < key_count)
+            for h in range(2):
+                query = qkv[k, h, 0:HD].astype(BF16)
+                key = jnp.transpose(qkv[k, h, HD : 2 * HD]).astype(BF16)
                 value = qkv[k, h, 2 * HD : 3 * HD].astype(BF16)
-                scores = dot_nn(query, key) / math.sqrt(HD)
+                scores = dot_nn(key, query) / math.sqrt(HD)
                 scores = jnp.where(keep, scores, -1e30)
-                raised = jnp.exp(scores - jnp.max(scores, axis=1, keepdims=True))
-                weights = (raised / jnp.sum(raised, axis=1, keepdims=True)).astype(BF16)
-                mixed = dot_nt(value, weights).astype(BF16)
-                pooled = (dot_nt(member, mixed) / got_float).astype(BF16)
-                term = term + dot_nn(pooled, wo[...])
-            terms.append(term)
+                raised = jnp.exp(scores - jnp.max(scores, axis=0, keepdims=True))
+                weights = (raised / jnp.sum(raised, axis=0, keepdims=True)).astype(BF16)
+                mixed = dot_nn(value, weights).astype(BF16)
+                heads[h].append(dot_nt(member, mixed) / got_float)
+        term = jnp.zeros((half, width), F32)
+        for pooled, wo in zip(heads, (w_out, w_out_peer)):
+            term = term + dot_nn(jnp.concatenate(pooled, axis=0).astype(BF16), wo[...])
         for k in range(images_here):
             for p in range(pieces):
-                part_f[pl.ds(k * pieces + p, NG, stride=packed), :] = terms[k][
-                    :, p * LANES : (p + 1) * LANES
+                part_f[pl.ds(k * pieces + p, NG, stride=packed), :] = term[
+                    k * NG : (k + 1) * NG, p * LANES : (p + 1) * LANES
                 ]
 
         part_b[...] = part_f[...].astype(BF16).reshape(NG, packed, LANES)
@@ -492,29 +507,33 @@
             norm = jnp.sum(jnp.where(inside, squares, 0.0), axis=0, keepdims=True)
             scale = jnp.where(inside, lax.rsqrt(norm + 1e-6), scale)
         own_unit = (pooled * scale).astype(BF16)
-        unit_box[...] = own_unit
         unit_in[place] = own_unit
 
-        def unit_copy(q):
+        def unit_y(step, at):
+            q = (y + step) % (2 * NYL)
             return pltpu.make_async_remote_copy(
-                src_ref=unit_box,
-                dst_ref=unit_in.at[place],
+                src_ref=unit_in.at[at],
+                dst_ref=unit_in.at[at],
                 send_sem=unit_send,
-                recv_sem=unit_recv,
-                device_id=(z * NYL + q // NG, (q % NG) * 2 + c),
-                device_id_type=MESH,
-            )
-
-        @pl.loop(0, 2 * NYL)
-        def _(j):
-            step = (j + 1) // 2
-            yy = (y + NYL + jnp.where(j % 2 == 1, 2 * NYL - step, step)) % (2 * NYL)
-            for i in (2, 1, 3, 0):
-                q = (yy % NYL) * NG + (yy // NYL) * NX + (x + i) % NX
-
-                @pl.when(q != place)
-                def _():
-                    unit_copy(q).start()
+                recv_sem=unit_recv.at[step],
+                device_id=(z * NYL + q % NYL, ((q // NYL) * NX + x) * 2 + c),
+                device_id_type=MESH,
+            )
+
+        def unit_x(at):
+            for i in (2, 1, 3):
+                pltpu.make_async_remote_copy(
+                    src_ref=unit_in.at[at],
+                    dst_ref=unit_in.at[at],
+                    send_sem=unit_send,
+                    recv_sem=unit_recv.at[0],
+                    device_id=(me, (yhi * NX + (x + i) % NX) * 2 + c),
+                    device_id_type=MESH,
+                ).start()
+
+        for step in (4, 3, 5, 2, 6, 1, 7):
+            unit_y(step, place).start()
+        unit_x(place)
 
         text_row = iota((text_rows, 1), 0)
         text_source = (text_row % nz) * NYL + ylo
@@ -533,14 +552,19 @@
         paired = (image_source == text_source) & (image_dest == pair_dest)
         labels = jnp.where(paired, 1.0, -1.0)
 
+        for step in (1, 7, 2, 6, 3, 5, 4):
+            q = (y + 2 * NYL - step) % (2 * NYL)
+            at = (q % NYL) * NG + (q // NYL) * NX + x
+            unit_y(step, at).wait_recv()
+            unit_x(at)
         pltpu.make_async_remote_copy(
-            src_ref=unit_in.at[pl.ds(0, plane - 1)],
-            dst_ref=unit_in.at[pl.ds(0, plane - 1)],
+            src_ref=unit_in.at[pl.ds(0, plane - 2 * NYL)],
+            dst_ref=unit_in.at[pl.ds(0, plane - 2 * NYL)],
             send_sem=unit_send,
-            recv_sem=unit_recv,
+            recv_sem=unit_recv.at[0],
             device_id=partner,
             device_id_type=MESH,
-        ).wait()
+        ).wait_recv()
         unit_wide[...] = unit_in[...].astype(F32).reshape(plane * packed, LANES)
         for yy in range(NYL):
             for k in range(images_here):
@@ -558,22 +582,26 @@
         turned = jnp.transpose(dscaled).astype(BF16)
         dscaled = dscaled.astype(BF16)
 
-        for xx in range(NX):
-            gi_box[xx] = dot_nn(turned, text_cols_b[:, xx * wide : (xx + 1) * wide]).astype(BF16)
-
-        def gi_copy(xx):
+        def gi_copy(n, xx):
             return pltpu.make_async_remote_copy(
-                src_ref=gi_box.at[xx],
-                dst_ref=gi_in.at[x],
-                send_sem=gi_send,
-                recv_sem=gi_recv,
+                src_ref=gi_box.at[n, xx],
+                dst_ref=gi_in.at[n, x],
+                send_sem=gi_send.at[n],
+                recv_sem=gi_recv.at[n],
                 device_id=(me, (yhi * NX + xx) * 2 + c),
                 device_id_type=MESH,
             )
 
-        for i in range(1, NX):
-            gi_copy(lax.rem(x + i, NX)).start()
-        gi_in[x] = gi_box[x]
+        pair_rows = 2 * half
+        for n in range(2):
+            for xx in range(NX):
+                gi_box[n, xx] = dot_nn(
+                    turned[n * pair_rows : (n + 1) * pair_rows],
+                    text_cols_b[:, xx * wide : (xx + 1) * wide],
+                ).astype(BF16)
+            for i in (2, 1, 3):
+                gi_copy(n, (x + i) % NX).start()
+            gi_in[n, x] = gi_box[n, x]
 
         text_grad = dot_nn(dscaled, units)
         for t in range(texts_here):
@@ -612,24 +640,6 @@
 
         gtz_in[z] = gt_box[z]
 
-        pltpu.make_async_remote_copy(
-            src_ref=gi_in.at[pl.ds(0, NX - 1)],
-            dst_ref=gi_in.at[pl.ds(0, NX - 1)],
-            send_sem=gi_send,
-            recv_sem=gi_recv,
-            device_id=partner,
-            device_id_type=MESH,
-        ).wait()
-        gi_sum[...] = jnp.sum(gi_in[...].astype(F32), axis=0)
-
-        for yy in range(2 * NYL):
-            for core in range(2):
-                q = (yy // NYL) * 2 + core
-                r = (yy % NYL) * half
-                gy_box[yy * 2 + core, 0:half, 0:HD] = gi_sum[
-                    r : r + half, q * HD : (q + 1) * HD
-                ].astype(BF16)
-
         def gy_copy(yy, core):
             return pltpu.make_async_remote_copy(
                 src_ref=gy_box.at[yy * 2 + core],
@@ -640,13 +650,28 @@
                 device_id_type=MESH,
             )
 
-        gy_copy(y, other).start()
-
-        @pl.loop(1, 2 * NYL)
-        def _(i):
-            yy = (y + i) % (2 * NYL)
-            gy_copy(yy, 0).start()
-            gy_copy(yy, 1).start()
+        for n in range(2):
+            pltpu.make_async_remote_copy(
+                src_ref=gi_in.at[n, pl.ds(0, NX - 1)],
+                dst_ref=gi_in.at[n, pl.ds(0, NX - 1)],
+                send_sem=gi_send.at[n],
+                recv_sem=gi_recv.at[n],
+                device_id=partner,
+                device_id_type=MESH,
+            ).wait()
+            gi_sum[...] = jnp.sum(gi_in[n].astype(F32), axis=0)
+            turn = [(row * NYL + 2 * n + r, core) for row in (0, 1) for r in (0, 1) for core in (0, 1)]
+            for yy, core in turn:
+                q = (yy // NYL) * 2 + core
+                r = (yy % 2) * half
+                gy_box[yy * 2 + core, :, 0:HD] = gi_sum[
+                    r : r + half, q * HD : (q + 1) * HD
+                ].astype(BF16)
+            for yy, core in turn:
+
+                @pl.when((yy != y) | (core != c))
+                def _():
+                    gy_copy(yy, core).start()
 
         gy_in[c * 2 * NYL + y] = gy_box[y * 2 + c]
 
@@ -674,7 +699,16 @@
         ).wait()
         for core in range(2):
             part = gy_in[core * 2 * NYL : (core + 1) * 2 * NYL].astype(F32)
-            grad_image[core * half : (core + 1) * half, :] = jnp.sum(part, axis=0)[0:half, 0:HD]
+            grad_image[core * half : (core + 1) * half, :] = jnp.sum(part, axis=0)[:, 0:HD]
+
+        pltpu.make_async_remote_copy(
+            src_ref=unit_in.at[pl.ds(0, plane - 1)],
+            dst_ref=unit_in.at[pl.ds(0, plane - 1)],
+            send_sem=unit_send,
+            recv_sem=unit_recv.at[0],
+            device_id=partner,
+            device_id_type=MESH,
+        ).wait_send()
 
         @pl.when(my_half == c)
         def _():
@@ -733,15 +767,14 @@
         pltpu.VMEM((NG, packed, LANES), BF16),
         pltpu.VMEM((NG, packed, LANES), BF16),
         pltpu.VMEM((packed, LANES), F32),
-        pltpu.VMEM((packed, LANES), BF16),
         pltpu.VMEM((plane, packed, LANES), BF16),
         pltpu.VMEM((plane * packed, LANES), F32),
         pltpu.VMEM((rows, width), F32),
-        pltpu.VMEM((NX, rows, wide), BF16),
-        pltpu.VMEM((NX, rows, wide), BF16),
-        pltpu.VMEM((rows, wide), F32),
-        pltpu.VMEM((4 * NYL, -(-half // 16) * 16, LANES), BF16),
-        pltpu.VMEM((4 * NYL, -(-half // 16) * 16, LANES), BF16),
+        pltpu.VMEM((2, NX, rows // 2, wide), BF16),
+        pltpu.VMEM((2, NX, rows // 2, wide), BF16),
+        pltpu.VMEM((rows // 2, wide), F32),
+        pltpu.VMEM((4 * NYL, half, LANES), BF16),
+        pltpu.VMEM((4 * NYL, half, LANES), BF16),
         pltpu.VMEM((2 * nz * packed, LANES), F32),
         pltpu.VMEM((nz * packed, LANES), F32),
         pltpu.VMEM((nz, packed, LANES), BF16),
@@ -760,9 +793,9 @@
         dma,
         dma,
         dma,
-        dma,
-        dma,
-        dma,
+        dma((2 * NYL,)),
+        dma((2,)),
+        dma((2,)),
         dma,
         dma,
         dma,

time: 77.8 us -> 75.9 us (0.976)
  Pallas kernels: 75 us -> 73.1 us
    pallas_call x1, Pallas kernels: 75 us -> 73.1 us  [on_device(): pl.pallas_call(kernel, out_shape=(jax.ShapeDtypeStruct((dp_size, HD), F32...]
where the time goes in v4:
time: 75.9 us; the launch traced here: 75.7 us
  Pallas kernels  73.1 us (96%)
  local copies, waits for them, and re-layouts  1.96 us (3%)
    pallas_call x1, Pallas kernels, on_device(): pl.pallas_call(kernel, out_shape=(jax.ShapeDtypeStruct((dp_size, HD), F32...  73.1 us
    unnamed x4, local copies, waits for them, and re-layouts  1.96 us

profile of v4, /device:TPU:1, one launch (start us, length us, event | category | flops | bytes accessed | tf_op | source)
XLA Modules:
  0.0 75.7 jit_solution(4645715543334432835)
XLA Ops:
  0.6 73.1 %shard_map.77 = (f32[48,72]{1,0:T(8,128)}, f32[3,1152]{1,0:T(4,128)}) custom-call(s32[18,128]{1,0:T(8,128)} %bitcast.4, s32[18,128]{1,0:T(8,128)} %bitcast.5, bf16[72,768]{1,0:T(8,128)(2,1)} %patches_in.1, bf16[216,1152]{1,0:T(8,128)(2,1)} %bitcast.3, bf16[72,1152]{1,0:T(8,128)(2,1)} %w_out_in.1, bf16[3,1152]{1,0:T(4,128)(2,1)} %text_arg.1), custom_call_target="tpu_custom_call" | custom-call | tf_op jit(solution)/shard_map/pallas_call | solution.py:815
  73.7 0.0 copy-start
  73.7 1.4 %copy.10 = f32[48,72]{1,0:T(8,128)} copy(f32[48,72]{1,0:T(8,128)} %get-tuple-element.4) | data formatting | bytes 27648
  75.1 0.0 copy-done
  75.1 0.6 copy.11
Async XLA Ops:
  73.7 1.4 %copy-start = (f32[3,1152]{1,0:T(4,128)S(1)}, f32[3,1152]{1,0:T(4,128)}, u32[]{:S(2)}) copy-start(f32[3,1152]{1,0:T(4,128)} %get-tuple-element.5) | copy-start | bytes 41476

commit v5 on v4

--- a/solution.py
+++ b/solution.py
@@ -70,7 +70,6 @@
         w_qkv_peer,
         w_out_peer,
         feats,
-        qkv,
         text_f,
         text_box,
         text_in,
@@ -394,6 +393,9 @@
         swap_qkv.wait()
         swap_out.wait()
 
+        row8, lane8 = iota((NG, LANES), 0), iota((NG, LANES), 1)
+        same = iota((LANES, LANES), 0) // MAXP == iota((LANES, LANES), 1) // MAXP
+        heads = ([], [])
         for k in range(images_here):
             feat_copy(k, own_row + far_x, left).wait_recv()
             for xx in (left_x, right_x, far_x):
@@ -402,8 +404,24 @@
             centred = full - jnp.sum(full, axis=0, keepdims=True) / width
             variance = jnp.sum(centred * centred, axis=0, keepdims=True) / width
             normed = (centred * lax.rsqrt(variance + 1e-6)).astype(BF16)
-            qkv[k, 0] = dot_nn(w_qkv[...], normed)
-            qkv[k, 1] = dot_nn(w_qkv_peer[...], normed)
+            got_k = got[k * NG : (k + 1) * NG]
+            got_float = got_k.astype(F32)
+            real = (lane8 // MAXP == row8) & (lane8 % MAXP < got_k)
+            member = real.astype(F32).astype(BF16)
+            key_count = jnp.broadcast_to(got_k.reshape(NG, 1, 1), (NG, MAXP, 1))
+            key_count = key_count.reshape(LANES, 1)
+            keep = same & (iota((LANES, 1), 0) % MAXP < key_count)
+            for h, wq in enumerate((w_qkv, w_qkv_peer)):
+                projected = dot_nn(wq[...], normed)
+                query = projected[0:HD].astype(BF16)
+                key = jnp.transpose(projected[HD : 2 * HD]).astype(BF16)
+                value = projected[2 * HD : 3 * HD].astype(BF16)
+                scores = dot_nn(key, query) / math.sqrt(HD)
+                scores = jnp.where(keep, scores, -1e30)
+                raised = jnp.exp(scores - jnp.max(scores, axis=0, keepdims=True))
+                weights = (raised / jnp.sum(raised, axis=0, keepdims=True)).astype(BF16)
+                mixed = dot_nn(value, weights).astype(BF16)
+                heads[h].append(dot_nt(member, mixed) / got_float)
         pltpu.make_async_remote_copy(
             src_ref=text_in.at[pl.ds(0, nz - 1)],
             dst_ref=text_in.at[pl.ds(0, nz - 1)],
@@ -413,27 +431,6 @@
             device_id_type=MESH,
         ).wait()
         text_swap.start()
-        row8, lane8 = iota((NG, LANES), 0), iota((NG, LANES), 1)
-        same = iota((LANES, LANES), 0) // MAXP == iota((LANES, LANES), 1) // MAXP
-        heads = ([], [])
-        for k in range(images_here):
-            got_k = got[k * NG : (k + 1) * NG]
-            got_float = got_k.astype(F32)
-            real = (lane8 // MAXP == row8) & (lane8 % MAXP < got_k)
-            member = real.astype(F32).astype(BF16)
-            key_count = jnp.broadcast_to(got_k.reshape(NG, 1, 1), (NG, MAXP, 1))
-            key_count = key_count.reshape(LANES, 1)
-            keep = same & (iota((LANES, 1), 0) % MAXP < key_count)
-            for h in range(2):
-                query = qkv[k, h, 0:HD].astype(BF16)
-                key = jnp.transpose(qkv[k, h, HD : 2 * HD]).astype(BF16)
-                value = qkv[k, h, 2 * HD : 3 * HD].astype(BF16)
-                scores = dot_nn(key, query) / math.sqrt(HD)
-                scores = jnp.where(keep, scores, -1e30)
-                raised = jnp.exp(scores - jnp.max(scores, axis=0, keepdims=True))
-                weights = (raised / jnp.sum(raised, axis=0, keepdims=True)).astype(BF16)
-                mixed = dot_nn(value, weights).astype(BF16)
-                heads[h].append(dot_nt(member, mixed) / got_float)
         term = jnp.zeros((half, width), F32)
         for pooled, wo in zip(heads, (w_out, w_out_peer)):
             term = term + dot_nn(jnp.concatenate(pooled, axis=0).astype(BF16), wo[...])
@@ -756,7 +753,6 @@
         pltpu.VMEM((3 * HD, width), BF16),
         pltpu.VMEM((HD, width), BF16),
         pltpu.VMEM((images_here, NG, 2 * HD, LANES), BF16),
-        pltpu.VMEM((images_here, 2, 3 * HD, LANES), F32),
         pltpu.VMEM((packed, LANES), F32),
         pltpu.VMEM((packed, LANES), BF16),
         pltpu.VMEM((2 * nz, packed, LANES), BF16),

time: 75.9 us -> 76.5 us (level)
  no operation moved by 1% of the time
where the time goes in v5:
time: 76.5 us; the launch traced here: 76.3 us
  Pallas kernels  73.7 us (96%)
  local copies, waits for them, and re-layouts  1.96 us (3%)
    pallas_call x1, Pallas kernels, on_device(): pl.pallas_call(kernel, out_shape=(jax.ShapeDtypeStruct((dp_size, HD), F32...  73.7 us
    unnamed x4, local copies, waits for them, and re-layouts  1.96 us

profile of v5, /device:TPU:1, one launch (start us, length us, event | category | flops | bytes accessed | tf_op | source)
XLA Modules:
  0.0 76.3 jit_solution(1641019310462486618)
XLA Ops:
  0.6 73.7 %shard_map.77 = (f32[48,72]{1,0:T(8,128)}, f32[3,1152]{1,0:T(4,128)}) custom-call(s32[18,128]{1,0:T(8,128)} %bitcast.4, s32[18,128]{1,0:T(8,128)} %bitcast.5, bf16[72,768]{1,0:T(8,128)(2,1)} %patches_in.1, bf16[216,1152]{1,0:T(8,128)(2,1)} %bitcast.3, bf16[72,1152]{1,0:T(8,128)(2,1)} %w_out_in.1, bf16[3,1152]{1,0:T(4,128)(2,1)} %text_arg.1), custom_call_target="tpu_custom_call" | custom-call | tf_op jit(solution)/shard_map/pallas_call | solution.py:811
  74.4 0.0 copy-start
  74.4 1.4 %copy.10 = f32[48,72]{1,0:T(8,128)} copy(f32[48,72]{1,0:T(8,128)} %get-tuple-element.4) | data formatting | bytes 27648
  75.7 0.0 copy-done
  75.7 0.6 copy.11
Async XLA Ops:
  74.4 1.4 %copy-start = (f32[3,1152]{1,0:T(4,128)S(1)}, f32[3,1152]{1,0:T(4,128)}, u32[]{:S(2)}) copy-start(f32[3,1152]{1,0:T(4,128)} %get-tuple-element.5) | copy-start | bytes 41476

commit v6 on v4

--- a/solution.py
+++ b/solution.py
@@ -455,9 +455,10 @@
                 device_id_type=MESH,
             )
 
-        @pl.loop(1, NG)
-        def _(i):
-            part_copy((g + i) % NG).start()
+        for row in (1 - yhi, yhi):
+            for i in (2, 1, 3):
+                part_copy(row * NX + (x + i) % NX).start()
+        part_copy(across).start()
 
         part_in[g] = part_b[g]
 
@@ -634,8 +635,7 @@
                 device_id_type=MESH,
             )
 
-        @pl.loop(1, nz)
-        def _(i):
+        for i in sorted(range(1, nz), key=lambda step: -min(step, nz - step)):
             gtz_copy(wrap(z + i, nz)).start()
 
         gtz_in[z] = gt_box[z]
@@ -822,15 +822,20 @@
         out_specs=(vmem, vmem),
         scratch_shapes=scratch,
         compiler_params=pltpu.CompilerParams(
-            collective_id=0, has_side_effects=True, vmem_limit_bytes=58 * 1024 * 1024
+            collective_id=0, has_side_effects=True, vmem_limit_bytes=40 * 1024 * 1024
         ),
     )(
-        counts.reshape(-1, LANES),
-        dest.reshape(-1, LANES),
-        patches,
-        w_qkv.reshape(3 * HD, width),
-        w_out,
-        text,
+        *(
+            pltpu.with_memory_space_constraint(array, pltpu.HBM)
+            for array in (
+                counts.reshape(-1, LANES),
+                dest.reshape(-1, LANES),
+                patches,
+                w_qkv.reshape(3 * HD, width),
+                w_out,
+                text,
+            )
+        )
     )
 
 

time: 75.9 us -> 73.2 us (0.964)
  Pallas kernels: 73.1 us -> 71.2 us
    pallas_call x1, Pallas kernels: 73.1 us -> 71.2 us  [on_device(): pl.pallas_call(kernel, out_shape=(jax.ShapeDtypeStruct((dp_size, HD), F32...]
    unnamed x4 -> x2, local copies, waits for them, and re-layouts: 1.96 us -> 1.22 us
where the time goes in v6:
time: 73.2 us; the launch traced here: 73 us
  Pallas kernels  71.2 us (97%)
  local copies, waits for them, and re-layouts  1.22 us (2%)
    pallas_call x1, Pallas kernels, on_device(): pl.pallas_call(kernel, out_shape=(jax.ShapeDtypeStruct((dp_size, HD), F32...  71.2 us

profile of v6, /device:TPU:1, one launch (start us, length us, event | category | flops | bytes accessed | tf_op | source)
XLA Modules:
  0.0 73.0 jit_solution(15823424832875159229)
XLA Ops:
  0.6 71.2 %shard_map.77 = (f32[48,72]{1,0:T(8,128)S(1)}, f32[3,1152]{1,0:T(4,128)S(1)}) custom-call(s32[18,128]{1,0:T(8,128)} %bitcast.4, s32[18,128]{1,0:T(8,128)} %bitcast.5, bf16[72,768]{1,0:T(8,128)(2,1)} %patches_in.1, bf16[216,1152]{1,0:T(8,128)(2,1)} %bitcast.3, bf16[72,1152]{1,0:T(8,128)(2,1)} %w_out_in.1, bf16[3,1152]{1,0:T(4,128)(2,1)} %text_arg.1), custom_call_target="tpu_custom_call" | custom-call | tf_op jit(solution)/shard_map/pallas_call | solution.py:815
  71.8 0.6 copy.10
  72.4 0.6 copy.11

commit v7 on v5

--- a/solution.py
+++ b/solution.py
@@ -70,6 +70,7 @@
         w_qkv_peer,
         w_out_peer,
         feats,
+        got_box,
         text_f,
         text_box,
         text_in,
@@ -186,8 +187,8 @@
         span = iota((dp_size, LANES), 1)
         order = iota((dp_size, LANES), 0)
         step = (order // NYL + 1) // 2
-        target = wrap(z + nz // 2 + jnp.where(order // NYL % 2 == 1, nz - step, step), nz)
-        target = wrap(target, nz) * NYL + (ylo + NYL - 1 - order % NYL) % NYL
+        target = wrap(z + jnp.where(order // NYL % 2 == 1, step, nz - step), nz)
+        target = target * NYL + (ylo + NYL - 1 - order % NYL) % NYL
         index = jnp.zeros((dp_size, 1), jnp.int32)
         base = first // LANES
         own_rows = []
@@ -215,7 +216,7 @@
                 src_ref=outbox.at[at],
                 dst_ref=inbox.at[c * half + my_slot],
                 send_sem=a2a_send,
-                recv_sem=a2a_recv,
+                recv_sem=a2a_recv.at[my_slot // NG],
                 device_id=(d, g * 2 + my_half),
                 device_id_type=MESH,
             )
@@ -235,24 +236,19 @@
             )
             if n == 0:
                 pl.semaphore_wait(barrier, total)
-            last = n == blocks - 1
-
-            @pl.loop(n * block_z, (n + 1) * block_z - (1 if last else 0))
+                for i in range(NYL - 1):
+                    image_copy(i, z * NYL + (ylo + NYL - 1 - i) % NYL).start()
+
+            @pl.loop(n * block_z + (1 if n == 0 else 0), (n + 1) * block_z)
             def _(j):
                 step = (j + 1) // 2
-                zz = wrap(z + nz // 2 + jnp.where(j % 2 == 1, nz - step, step), nz)
-                zz = wrap(zz, nz)
+                zz = wrap(z + jnp.where(j % 2 == 1, step, nz - step), nz)
                 for i in range(NYL):
                     d = zz * NYL + (ylo + NYL - 1 - i) % NYL
                     image_copy(j * NYL + i, d).start()
 
-            if last:
-                for i in range(NYL - 1):
-                    d = z * NYL + (ylo + NYL - 1 - i) % NYL
-                    image_copy((nz - 1) * NYL + i, d).start()
-
         own_copy = pltpu.make_async_copy(
-            outbox.at[dp_size - 1], inbox.at[c * half + my_slot], local_sem
+            outbox.at[NYL - 1], inbox.at[c * half + my_slot], local_sem
         )
 
         @pl.when(my_half == c)
@@ -261,7 +257,7 @@
 
         @pl.when(my_half != c)
         def _():
-            image_copy(dp_size - 1, me).start()
+            image_copy(NYL - 1, me).start()
 
         def swap(src, dst, i):
             return pltpu.make_async_remote_copy(
@@ -321,32 +317,58 @@
             row = pl.ds(half_rows * c + r, 1)
             inside = (r * LANES + slot_lane) // dp_size == slot_row
             got = got + jnp.where(inside & (dest[row, :] == me), counts[row, :], 0)
-        got = jnp.sum(got, axis=1, keepdims=True)
-
-        @pl.when(my_half == c)
-        def _():
-            own_copy.wait()
-            pltpu.make_async_remote_copy(
-                src_ref=inbox.at[pl.ds(0, 2 * half - 1)],
-                dst_ref=inbox.at[pl.ds(0, 2 * half - 1)],
-                send_sem=a2a_send,
-                recv_sem=a2a_recv,
-                device_id=partner,
-                device_id_type=MESH,
-            ).wait_recv()
-
-        @pl.when(my_half != c)
-        def _():
-            pltpu.make_async_remote_copy(
-                src_ref=inbox,
-                dst_ref=inbox,
-                send_sem=a2a_send,
-                recv_sem=a2a_recv,
-                device_id=partner,
-                device_id_type=MESH,
-            ).wait_recv()
-
+        got_box[...] = jnp.broadcast_to(jnp.sum(got, axis=1, keepdims=True), (half, LANES))
+
+        def near_first(core):
+            if images_here == 1:
+                return [0]
+            away = []
+            for k in range(images_here):
+                gap = jnp.abs(2 * z - (core * nz + 4 * k + 1))
+                away.append(jnp.minimum(gap, 2 * nz - gap))
+            d0, d1, d2 = away
+            nearest = jnp.where(
+                d0 < d1, jnp.where(d0 < d2, 0, 2), jnp.where(d1 < d2, 1, 2)
+            )
+            farthest = jnp.where(
+                d0 > d1, jnp.where(d0 > d2, 0, 2), jnp.where(d1 > d2, 1, 2)
+            )
+            return [nearest, 3 - nearest - farthest, farthest]
+
+        chunk_of = near_first(c)
         eye = (iota((HD, HD), 0) == iota((HD, HD), 1)).astype(F32).astype(BF16)
+
+        def arrive(k):
+            chunk = chunk_of[k]
+            holds_own = (my_half == c) & (my_slot // NG == chunk)
+
+            def wait_images(many):
+                pltpu.make_async_remote_copy(
+                    src_ref=inbox.at[pl.ds(0, many)],
+                    dst_ref=inbox.at[pl.ds(0, many)],
+                    send_sem=a2a_send,
+                    recv_sem=a2a_recv.at[chunk],
+                    device_id=partner,
+                    device_id_type=MESH,
+                ).wait_recv()
+
+            @pl.when(holds_own)
+            def _():
+                own_copy.wait()
+                wait_images(2 * NG - 1)
+
+            @pl.when(jnp.logical_not(holds_own))
+            def _():
+                wait_images(2 * NG)
+
+            low, high = (
+                dot_nt(eye, inbox[pl.ds(r + chunk * NG, NG)].reshape(LANES, HD))
+                for r in (0, half)
+            )
+            feats[k, g] = jnp.concatenate([low, high], axis=0).astype(BF16)
+            feat_copy(k, g, across).start()
+            feat_copy(k, g, left).start()
+            feat_copy(k, g, right).start()
 
         across = (1 - yhi) * NX + x
         left_x, right_x = lax.rem(x + NX - 1, NX), lax.rem(x + 1, NX)
@@ -364,39 +386,31 @@
 
         own_row, far_row = yhi * NX, (1 - yhi) * NX
         left, right = own_row + left_x, own_row + right_x
-        for k in range(images_here):
-            low, high = (
-                dot_nt(eye, inbox[r + k * NG : r + (k + 1) * NG].reshape(LANES, HD))
-                for r in (0, half)
-            )
-            feats[k, g] = jnp.concatenate([low, high], axis=0).astype(BF16)
-            feat_copy(k, g, across).start()
-            feat_copy(k, g, left).start()
-            feat_copy(k, g, right).start()
-
-        @pl.loop(1, nz)
-        def _(i):
-            text_copy(wrap(z + i, nz)).start()
-
-        for k in range(images_here):
+        def pass_row(k):
             feat_copy(k, left, left).wait_recv()
             if k % 2 == 0:
                 feat_copy(k, left, right).start()
             feat_copy(k, right, left).wait_recv()
             if k % 2 == 1:
                 feat_copy(k, right, left).start()
+
+        def pass_across(k):
             feat_copy(k, across, across).wait_recv()
             feat_copy(k, across, own_row + far_x).start()
             feat_copy(k, across, left).start()
             feat_copy(k, across, right).start()
 
-        swap_qkv.wait()
-        swap_out.wait()
+        def send_texts():
+            @pl.loop(1, nz)
+            def _(i):
+                text_copy(wrap(z + i, nz)).start()
 
         row8, lane8 = iota((NG, LANES), 0), iota((NG, LANES), 1)
         same = iota((LANES, LANES), 0) // MAXP == iota((LANES, LANES), 1) // MAXP
         heads = ([], [])
-        for k in range(images_here):
+        got_now = []
+
+        def attend(k):
             feat_copy(k, own_row + far_x, left).wait_recv()
             for xx in (left_x, right_x, far_x):
                 feat_copy(k, far_row + xx, left).wait_recv()
@@ -404,7 +418,8 @@
             centred = full - jnp.sum(full, axis=0, keepdims=True) / width
             variance = jnp.sum(centred * centred, axis=0, keepdims=True) / width
             normed = (centred * lax.rsqrt(variance + 1e-6)).astype(BF16)
-            got_k = got[k * NG : (k + 1) * NG]
+            got_k = got_box[pl.ds(pl.multiple_of(chunk_of[k] * NG, NG), NG), 0:1]
+            got_now.append(got_k)
             got_float = got_k.astype(F32)
             real = (lane8 // MAXP == row8) & (lane8 % MAXP < got_k)
             member = real.astype(F32).astype(BF16)
@@ -422,6 +437,28 @@
                 weights = (raised / jnp.sum(raised, axis=0, keepdims=True)).astype(BF16)
                 mixed = dot_nn(value, weights).astype(BF16)
                 heads[h].append(dot_nt(member, mixed) / got_float)
+
+        arrive(0)
+        if images_here == 3:
+            arrive(1)
+            pass_row(0)
+            pass_across(0)
+            arrive(2)
+            send_texts()
+            pass_row(1)
+            pass_across(1)
+        else:
+            send_texts()
+            pass_row(0)
+            pass_across(0)
+        swap_qkv.wait()
+        swap_out.wait()
+        attend(0)
+        if images_here == 3:
+            pass_row(2)
+            pass_across(2)
+            attend(1)
+            attend(2)
         pltpu.make_async_remote_copy(
             src_ref=text_in.at[pl.ds(0, nz - 1)],
             dst_ref=text_in.at[pl.ds(0, nz - 1)],
@@ -452,16 +489,17 @@
                 device_id_type=MESH,
             )
 
-        @pl.loop(1, NG)
-        def _(i):
-            part_copy((g + i) % NG).start()
+        for row in (1 - yhi, yhi):
+            for i in (2, 1, 3):
+                part_copy(row * NX + (x + i) % NX).start()
+        part_copy(across).start()
 
         part_in[g] = part_b[g]
 
         here = (lane8 // MAXP == g).astype(F32).astype(BF16)
         for k in range(images_here):
             own_got = jnp.sum(
-                jnp.where(iota((NG, 1), 0) == g, got[k * NG : (k + 1) * NG], 0),
+                jnp.where(iota((NG, 1), 0) == g, got_now[k], 0),
                 axis=0,
                 keepdims=True,
             ).astype(F32)
@@ -544,7 +582,11 @@
             )
         pair_dest = jnp.sum(pair_dest, axis=1, keepdims=True)
         image_lane = iota((text_rows, rows), 1)
-        image_source = c * half + image_lane % half
+        image_source = c * half + image_lane % NG
+        for k in range(images_here):
+            image_source = image_source + jnp.where(
+                image_lane % half // NG == k, chunk_of[k] * NG, 0
+            )
         image_dest = z * NYL + image_lane // half
         paired = (image_source == text_source) & (image_dest == pair_dest)
         labels = jnp.where(paired, 1.0, -1.0)
@@ -631,8 +673,7 @@
                 device_id_type=MESH,
             )
 
-        @pl.loop(1, nz)
-        def _(i):
+        for i in sorted(range(1, nz), key=lambda step: -min(step, nz - step)):
             gtz_copy(wrap(z + i, nz)).start()
 
         gtz_in[z] = gt_box[z]
@@ -696,7 +737,10 @@
         ).wait()
         for core in range(2):
             part = gy_in[core * 2 * NYL : (core + 1) * 2 * NYL].astype(F32)
-            grad_image[core * half : (core + 1) * half, :] = jnp.sum(part, axis=0)[:, 0:HD]
+            part = jnp.sum(part, axis=0)
+            for k, chunk in enumerate(near_first(core)):
+                row = pl.multiple_of(core * half + chunk * NG, NG)
+                grad_image[pl.ds(row, NG), :] = part[k * NG : (k + 1) * NG, 0:HD]
 
         pltpu.make_async_remote_copy(
             src_ref=unit_in.at[pl.ds(0, plane - 1)],
@@ -713,7 +757,7 @@
                 src_ref=outbox.at[pl.ds(0, dp_size - 1)],
                 dst_ref=outbox.at[pl.ds(0, dp_size - 1)],
                 send_sem=a2a_send,
-                recv_sem=a2a_recv,
+                recv_sem=a2a_recv.at[0],
                 device_id=partner,
                 device_id_type=MESH,
             ).wait_send()
@@ -724,7 +768,7 @@
                 src_ref=outbox,
                 dst_ref=outbox,
                 send_sem=a2a_send,
-                recv_sem=a2a_recv,
+                recv_sem=a2a_recv.at[0],
                 device_id=partner,
                 device_id_type=MESH,
             ).wait_send()
@@ -753,6 +797,7 @@
         pltpu.VMEM((3 * HD, width), BF16),
         pltpu.VMEM((HD, width), BF16),
         pltpu.VMEM((images_here, NG, 2 * HD, LANES), BF16),
+        pltpu.VMEM((half, LANES), jnp.int32),
         pltpu.VMEM((packed, LANES), F32),
         pltpu.VMEM((packed, LANES), BF16),
         pltpu.VMEM((2 * nz, packed, LANES), BF16),
@@ -777,7 +822,7 @@
         pltpu.VMEM((nz, packed, LANES), BF16),
         dma,
         dma,
-        dma,
+        dma((images_here,)),
         dma((2,)),
         dma((2,)),
         dma((images_here,)),
@@ -818,15 +863,20 @@
         out_specs=(vmem, vmem),
         scratch_shapes=scratch,
         compiler_params=pltpu.CompilerParams(
-            collective_id=0, has_side_effects=True, vmem_limit_bytes=58 * 1024 * 1024
+            collective_id=0, has_side_effects=True, vmem_limit_bytes=40 * 1024 * 1024
         ),
     )(
-        counts.reshape(-1, LANES),
-        dest.reshape(-1, LANES),
-        patches,
-        w_qkv.reshape(3 * HD, width),
-        w_out,
-        text,
+        *(
+            pltpu.with_memory_space_constraint(array, pltpu.HBM)
+            for array in (
+                counts.reshape(-1, LANES),
+                dest.reshape(-1, LANES),
+                patches,
+                w_qkv.reshape(3 * HD, width),
+                w_out,
+                text,
+            )
+        )
     )
 
 

time: 76.5 us -> 74 us (0.967)
  Pallas kernels: 73.7 us -> 72 us
    pallas_call x1, Pallas kernels: 73.7 us -> 72 us  [on_device(): pl.pallas_call(kernel, out_shape=(jax.ShapeDtypeStruct((dp_size, HD), F32...]
    unnamed x4 -> x2, local copies, waits for them, and re-layouts: 1.96 us -> 1.22 us
where the time goes in v7:
time: 74 us; the launch traced here: 73.9 us
  Pallas kernels  72 us (97%)
  local copies, waits for them, and re-layouts  1.22 us (2%)
    pallas_call x1, Pallas kernels, on_device(): pl.pallas_call(kernel, out_shape=(jax.ShapeDtypeStruct((dp_size, HD), F32...  72 us

profile of v7, /device:TPU:1, one launch (start us, length us, event | category | flops | bytes accessed | tf_op | source)
XLA Modules:
  0.0 73.9 jit_solution(12147625588090121706)
XLA Ops:
  0.6 72.0 %shard_map.77 = (f32[48,72]{1,0:T(8,128)S(1)}, f32[3,1152]{1,0:T(4,128)S(1)}) custom-call(s32[18,128]{1,0:T(8,128)} %bitcast.4, s32[18,128]{1,0:T(8,128)} %bitcast.5, bf16[72,768]{1,0:T(8,128)(2,1)} %patches_in.1, bf16[216,1152]{1,0:T(8,128)(2,1)} %bitcast.3, bf16[72,1152]{1,0:T(8,128)(2,1)} %w_out_in.1, bf16[3,1152]{1,0:T(4,128)(2,1)} %text_arg.1), custom_call_target="tpu_custom_call" | custom-call | tf_op jit(solution)/shard_map/pallas_call | solution.py:856
  72.7 0.6 copy.10
  73.3 0.6 copy.11

commit v8 on v6

--- a/solution.py
+++ b/solution.py
@@ -142,9 +142,6 @@
                 )
             )
         ]
-        for load in loads:
-            load.start()
-
         barrier = pltpu.get_barrier_semaphore()
 
         def greet(device):
@@ -160,6 +157,9 @@
                 greet((src, mp))
 
         greet(partner)
+
+        for load in loads:
+            load.start()
 
         @pl.loop(1, nz)
         def _(i):
@@ -222,35 +222,23 @@
             )
 
         total = (2 * half - 1 + extra) + 1 + (nz - 1) + 2 * (2 * NYL - 1) + 2 * (NX - 1)
-        blocks = 4
-        block_rows = slots // blocks
-        block_images = dp_size // blocks
-        block_z = nz // blocks
-        for n in range(blocks):
-            chosen = iota((block_rows, patches.shape[1]), 1) == column[
-                n * block_rows : (n + 1) * block_rows
-            ]
-            picked = dot_nt(chosen.astype(F32).astype(BF16), patches[...]).astype(BF16)
-            outbox[n * block_images : (n + 1) * block_images] = picked.reshape(
-                block_images, MAXP, HD
-            )
-            if n == 0:
-                pl.semaphore_wait(barrier, total)
-            last = n == blocks - 1
-
-            @pl.loop(n * block_z, (n + 1) * block_z - (1 if last else 0))
-            def _(j):
-                step = (j + 1) // 2
-                zz = wrap(z + nz // 2 + jnp.where(j % 2 == 1, nz - step, step), nz)
-                zz = wrap(zz, nz)
-                for i in range(NYL):
-                    d = zz * NYL + (ylo + NYL - 1 - i) % NYL
-                    image_copy(j * NYL + i, d).start()
-
-            if last:
-                for i in range(NYL - 1):
-                    d = z * NYL + (ylo + NYL - 1 - i) % NYL
-                    image_copy((nz - 1) * NYL + i, d).start()
+        chosen = iota((slots, patches.shape[1]), 1) == column
+        picked = dot_nt(chosen.astype(F32).astype(BF16), patches[...]).astype(BF16)
+        outbox[...] = picked.reshape(dp_size, MAXP, HD)
+        pl.semaphore_wait(barrier, total)
+
+        @pl.loop(0, nz - 1)
+        def _(j):
+            step = (j + 1) // 2
+            zz = wrap(z + nz // 2 + jnp.where(j % 2 == 1, nz - step, step), nz)
+            zz = wrap(zz, nz)
+            for i in range(NYL):
+                d = zz * NYL + (ylo + NYL - 1 - i) % NYL
+                image_copy(j * NYL + i, d).start()
+
+        for i in range(NYL - 1):
+            d = z * NYL + (ylo + NYL - 1 - i) % NYL
+            image_copy((nz - 1) * NYL + i, d).start()
 
         own_copy = pltpu.make_async_copy(
             outbox.at[dp_size - 1], inbox.at[c * half + my_slot], local_sem
@@ -428,11 +416,11 @@
                 query = qkv[k, h, 0:HD].astype(BF16)
                 key = jnp.transpose(qkv[k, h, HD : 2 * HD]).astype(BF16)
                 value = qkv[k, h, 2 * HD : 3 * HD].astype(BF16)
-                scores = dot_nn(key, query) / math.sqrt(HD)
+                scores = dot_nn(key, query) * (1.0 / math.sqrt(HD))
                 scores = jnp.where(keep, scores, -1e30)
                 raised = jnp.exp(scores - jnp.max(scores, axis=0, keepdims=True))
-                weights = (raised / jnp.sum(raised, axis=0, keepdims=True)).astype(BF16)
-                mixed = dot_nn(value, weights).astype(BF16)
+                mixed = dot_nn(value, raised.astype(BF16))
+                mixed = (mixed / jnp.sum(raised, axis=0, keepdims=True)).astype(BF16)
                 heads[h].append(dot_nt(member, mixed) / got_float)
         term = jnp.zeros((half, width), F32)
         for pooled, wo in zip(heads, (w_out, w_out_peer)):

time: 73.2 us -> 73 us (level)
  no operation moved by 1% of the time
where the time goes in v8:
time: 73 us; the launch traced here: 72.8 us
  Pallas kernels  71 us (97%)
  local copies, waits for them, and re-layouts  1.22 us (2%)
    pallas_call x1, Pallas kernels, on_device(): pl.pallas_call(kernel, out_shape=(jax.ShapeDtypeStruct((dp_size, HD), F32...  71 us

profile of v8, /device:TPU:1, one launch (start us, length us, event | category | flops | bytes accessed | tf_op | source)
XLA Modules:
  0.0 72.8 jit_solution(3375181513772296197)
XLA Ops:
  0.6 71.0 %shard_map.77 = (f32[48,72]{1,0:T(8,128)S(1)}, f32[3,1152]{1,0:T(4,128)S(1)}) custom-call(s32[18,128]{1,0:T(8,128)} %bitcast.4, s32[18,128]{1,0:T(8,128)} %bitcast.5, bf16[72,768]{1,0:T(8,128)(2,1)} %patches_in.1, bf16[216,1152]{1,0:T(8,128)(2,1)} %bitcast.3, bf16[72,1152]{1,0:T(8,128)(2,1)} %w_out_in.1, bf16[3,1152]{1,0:T(4,128)(2,1)} %text_arg.1), custom_call_target="tpu_custom_call" | custom-call | tf_op jit(solution)/shard_map/pallas_call | solution.py:803
  71.6 0.6 copy.10
  72.2 0.6 copy.11

commit v9 on v6

--- a/solution.py
+++ b/solution.py
@@ -594,7 +594,7 @@
             )
 
         pair_rows = 2 * half
-        for n in range(2):
+        def send_half(n):
             for xx in range(NX):
                 gi_box[n, xx] = dot_nn(
                     turned[n * pair_rows : (n + 1) * pair_rows],
@@ -603,6 +603,8 @@
             for i in (2, 1, 3):
                 gi_copy(n, (x + i) % NX).start()
             gi_in[n, x] = gi_box[n, x]
+
+        send_half(0)
 
         text_grad = dot_nn(dscaled, units)
         for t in range(texts_here):
@@ -620,6 +622,7 @@
             device_id_type=MESH,
         )
         gt_copy.start()
+        send_half(1)
 
         gt_copy.wait()
         own_sums = gt_f[pl.ds(pl.multiple_of(c * core_rows, 8), core_rows), :]

time: 73.2 us -> 73.1 us (level)
  no operation moved by 1% of the time
where the time goes in v9:
time: 73.1 us; the launch traced here: 73 us
  Pallas kernels  71.1 us (97%)
  local copies, waits for them, and re-layouts  1.22 us (2%)
    pallas_call x1, Pallas kernels, on_device(): pl.pallas_call(kernel, out_shape=(jax.ShapeDtypeStruct((dp_size, HD), F32...  71.1 us

profile of v9, /device:TPU:1, one launch (start us, length us, event | category | flops | bytes accessed | tf_op | source)
XLA Modules:
  0.0 73.0 jit_solution(7416252179462556291)
XLA Ops:
  0.6 71.1 %shard_map.77 = (f32[48,72]{1,0:T(8,128)S(1)}, f32[3,1152]{1,0:T(4,128)S(1)}) custom-call(s32[18,128]{1,0:T(8,128)} %bitcast.4, s32[18,128]{1,0:T(8,128)} %bitcast.5, bf16[72,768]{1,0:T(8,128)(2,1)} %patches_in.1, bf16[216,1152]{1,0:T(8,128)(2,1)} %bitcast.3, bf16[72,1152]{1,0:T(8,128)(2,1)} %w_out_in.1, bf16[3,1152]{1,0:T(4,128)(2,1)} %text_arg.1), custom_call_target="tpu_custom_call" | custom-call | tf_op jit(solution)/shard_map/pallas_call | solution.py:818
  71.8 0.6 copy.10
  72.4 0.6 copy.11

commit v10 on v9

--- a/solution.py
+++ b/solution.py
@@ -443,7 +443,7 @@
                     k * NG : (k + 1) * NG, p * LANES : (p + 1) * LANES
                 ]
 
-        part_b[...] = part_f[...].astype(BF16).reshape(NG, packed, LANES)
+        part_b[...] = part_f[0 : NG * packed].astype(BF16).reshape(NG, packed, LANES)
 
         def part_copy(gg):
             return pltpu.make_async_remote_copy(
@@ -475,7 +475,7 @@
                 mean_f[r : r + 1, :] = mean[0:1, p * LANES : (p + 1) * LANES]
 
         text_swap.wait()
-        text_wide[...] = text_in[...].astype(F32).reshape(2 * nz * packed, LANES)
+        text_wide[0 : 2 * nz * packed] = text_in[...].astype(F32).reshape(-1, LANES)
         for t in range(texts_here):
             for p in range(pieces):
                 text_full[t * 2 * nz : (t + 1) * 2 * nz, p * LANES : (p + 1) * LANES] = (
@@ -566,7 +566,7 @@
             device_id=partner,
             device_id_type=MESH,
         ).wait_recv()
-        unit_wide[...] = unit_in[...].astype(F32).reshape(plane * packed, LANES)
+        unit_wide[0 : plane * packed] = unit_in[...].astype(F32).reshape(-1, LANES)
         for yy in range(NYL):
             for k in range(images_here):
                 for p in range(pieces):
@@ -763,22 +763,22 @@
         pltpu.VMEM((packed, LANES), F32),
         pltpu.VMEM((packed, LANES), BF16),
         pltpu.VMEM((2 * nz, packed, LANES), BF16),
-        pltpu.VMEM((2 * nz * packed, LANES), F32),
+        pltpu.VMEM(((2 * nz + 1) * packed, LANES), F32),
         pltpu.VMEM((text_rows, width), F32),
         pltpu.VMEM((text_rows, NX * wide), F32),
-        pltpu.VMEM((NG * packed, LANES), F32),
+        pltpu.VMEM(((NG + 1) * packed, LANES), F32),
         pltpu.VMEM((NG, packed, LANES), BF16),
         pltpu.VMEM((NG, packed, LANES), BF16),
         pltpu.VMEM((packed, LANES), F32),
         pltpu.VMEM((plane, packed, LANES), BF16),
-        pltpu.VMEM((plane * packed, LANES), F32),
+        pltpu.VMEM(((plane + 1) * packed, LANES), F32),
         pltpu.VMEM((rows, width), F32),
         pltpu.VMEM((2, NX, rows // 2, wide), BF16),
         pltpu.VMEM((2, NX, rows // 2, wide), BF16),
         pltpu.VMEM((rows // 2, wide), F32),
         pltpu.VMEM((4 * NYL, half, LANES), BF16),
         pltpu.VMEM((4 * NYL, half, LANES), BF16),
-        pltpu.VMEM((2 * nz * packed, LANES), F32),
+        pltpu.VMEM(((2 * nz + 1) * packed, LANES), F32),
         pltpu.VMEM((nz * packed, LANES), F32),
         pltpu.VMEM((nz, packed, LANES), BF16),
         pltpu.VMEM((nz, packed, LANES), BF16),

time: 73.1 us -> 73.1 us (level)
  no operation moved by 1% of the time
where the time goes in v10:
time: 73.1 us; the launch traced here: 73 us
  Pallas kernels  71.1 us (97%)
  local copies, waits for them, and re-layouts  1.22 us (2%)
    pallas_call x1, Pallas kernels, on_device(): pl.pallas_call(kernel, out_shape=(jax.ShapeDtypeStruct((dp_size, HD), F32...  71.1 us

profile of v10, /device:TPU:1, one launch (start us, length us, event | category | flops | bytes accessed | tf_op | source)
XLA Modules:
  0.0 73.0 jit_solution(5754536282053057925)
XLA Ops:
  0.6 71.1 %shard_map.77 = (f32[48,72]{1,0:T(8,128)S(1)}, f32[3,1152]{1,0:T(4,128)S(1)}) custom-call(s32[18,128]{1,0:T(8,128)} %bitcast.4, s32[18,128]{1,0:T(8,128)} %bitcast.5, bf16[72,768]{1,0:T(8,128)(2,1)} %patches_in.1, bf16[216,1152]{1,0:T(8,128)(2,1)} %bitcast.3, bf16[72,1152]{1,0:T(8,128)(2,1)} %w_out_in.1, bf16[3,1152]{1,0:T(4,128)(2,1)} %text_arg.1), custom_call_target="tpu_custom_call" | custom-call | tf_op jit(solution)/shard_map/pallas_call | solution.py:818
  71.8 0.6 copy.10
  72.4 0.6 copy.11
